TPU v7x, 128 devices: a whole 4x4x4 slice. The times are simulated.
128 devices in a mesh: dp: 32 (over y, x, core), tensor: 4 (over z).
Axes of the slice: x: 4, y: 4, z: 4, core: 2. Of those that a mesh axis runs over, the one named last changes fastest.
Arguments:
- tokens: bfloat16 [6, 16384, 4096], P(None, 'dp', 'tensor'), may hold values from -16 to 16
- router: bfloat16 [16, 4096], P(None, 'tensor'), may hold values from -32 to 32
- w_gate: bfloat16 [4, 14336, 4096], P('tensor', 'dp'), may hold values from -0.625 to 0.625
- w_up: bfloat16 [4, 14336, 4096], P('tensor', 'dp'), may hold values from -0.625 to 0.625
- w_down: bfloat16 [4, 14336, 4096], P('tensor', 'dp'), may hold values from -0.046875 to 0.046875
Outputs:
- mixed: bfloat16 [6, 16384, 4096], P(None, 'dp', 'tensor')
- log_total: float32 [6, 16384], P(None, 'dp')
All inputs are finite; a program needn't handle non-finite values.
Results may differ from a plain program's by a relative error of at most 0.0096.
Values may be sent and summed in bfloat16 or wider, within the bound.
No kernel may reach another device: no remote copies, remote signals or barrier semaphores. Data moves between devices by JAX's collectives and lax.ppermute only.
A program may use at most 128 MiB of HBM per device.

v0:
```python
import jax
import jax.numpy as jnp
from jax import lax
from jax.sharding import PartitionSpec as P

SLOTS = 4


epsilon = 1e-05


def per_device(tokens, router, w_gate, w_up, w_down):
    width_part = tokens.shape[2]
    tensor_count = lax.axis_size("tensor")
    full_width = width_part * tensor_count
    squares = jnp.sum(jnp.square(tokens.astype(jnp.float32)), axis=2)
    raw_logits = jnp.einsum("sd,gtd->gst", router, tokens, preferred_element_type=jnp.float32)
    raw_logits, squares = lax.psum((raw_logits, squares), "tensor")
    norm_scale = lax.rsqrt(squares / full_width + epsilon)
    logits = raw_logits * norm_scale[:, None, :]
    peaks = lax.pmax(jnp.max(logits, axis=2), "dp")
    powers = jnp.exp(logits - peaks[:, :, None])
    local_sum = jnp.sum(powers, axis=2)
    weights = (powers * norm_scale[:, None, :]).astype(jnp.bfloat16)
    partial_value = jnp.einsum("gst,gtd->gsd", weights, tokens, preferred_element_type=jnp.float32)
    column_sum = lax.psum(local_sum, "dp")
    slot_in = lax.psum(partial_value / column_sum[:, :, None], "dp").astype(jnp.bfloat16)
    row_peak = jnp.max(logits, axis=1, keepdims=True)
    row_powers = jnp.exp(logits - row_peak)
    row_sum = jnp.sum(row_powers, axis=1, keepdims=True)
    combine = (row_powers / row_sum).astype(jnp.bfloat16)
    log_total = (row_peak + jnp.log(row_sum))[:, 0, :]
    experts_here = w_gate.shape[0]
    inputs = lax.all_to_all(slot_in, "tensor", split_axis=1, concat_axis=2, tiled=True)
    count = inputs.shape[0]
    grouped = inputs.reshape(count, experts_here, SLOTS, full_width)
    gate_act = jnp.einsum("nksd,kfd->nksf", grouped, w_gate, preferred_element_type=jnp.float32)
    up_act = jnp.einsum("nksd,kfd->nksf", grouped, w_up, preferred_element_type=jnp.float32)
    hidden = (jax.nn.silu(gate_act) * up_act).astype(jnp.bfloat16)
    result = jnp.einsum("nksf,kfd->nksd", hidden, w_down, preferred_element_type=jnp.float32)
    partial_out = result.reshape(count, experts_here * SLOTS, full_width)
    slot_out = lax.psum(partial_out, "dp").astype(jnp.bfloat16)
    window_out = lax.all_to_all(slot_out, "tensor", split_axis=2, concat_axis=1, tiled=True)
    mixed = jnp.einsum(
        "gst,gsd->gtd", combine, window_out, preferred_element_type=jnp.float32
    ).astype(jnp.bfloat16)
    return (mixed, log_total)


def solution(mesh):
    in_specs = (
        P(None, "dp", "tensor"),
        P(None, "tensor"),
        P("tensor", "dp", None),
        P("tensor", "dp", None),
        P("tensor", "dp", None),
    )
    out_specs = (P(None, "dp", "tensor"), P(None, "dp"))
    return jax.shard_map(
        per_device, mesh=mesh, in_specs=in_specs, out_specs=out_specs, check_vma=False
    )
```

profile of v0, /device:TPU:1, one launch (start us, length us, event | category | flops | bytes accessed | tf_op | source)
XLA Modules:
  0.0 509.4 jit_solution(3205475498127815462)
XLA Ops:
  7.2 0.7 copy-done
  7.9 5.2 %convolution_bitcast_fusion = f32[6,16,512]{2,1,0:T(8,128)} fusion(bf16[6,512,1024]{2,1,0:T(8,128)(2,1)} %param.5, bf16[16,1024]{1,0:T(8,128)(2,1)S(1)} %copy-done), kind=kOutput, calls=%fused_computation.9 | convolution fusion | flops 100663296 | bytes 6520832 | tf_op jit(solution)/shard_map/sd,gtd->gst/dot_general | solution.py:17
  13.2 4.1 multiply_reduce_fusion
  17.2 15.2 %psum.36 = f32[6,512]{1,0:T(8,128)S(1)} all-reduce(f32[6,512]{1,0:T(8,128)S(1)} %multiply_reduce_fusion), channel_id=1, replica_groups=mesh['dp'=32,'tensor'=4] {'tensor'}, use_global_device_ids=true, to_apply=%region_2.0 | all-reduce | flops 3072 | bytes 24576 | tf_op jit(solution)/shard_map/psum | solution.py:18
  32.5 23.6 %all-reduce.4.cloned.1.call-done = f32[6,16,512]{2,1,0:T(8,128)} async-done(((f32[6,16,512]{2,1,0:T(8,128)}), f32[6,16,512]{2,1,0:T(8,128)}) %all-reduce.4.cloned.1.call-update) | async-done | bytes 196624 | tf_op jit(solution)/shard_map/psum | solution.py:18
  56.1 1.0 multiply_reduce_fusion.2
  57.1 1.0 fusion.23
  58.2 64.8 %pmax.7 = f32[6,16]{1,0:T(8,128)S(1)} all-reduce(f32[6,16]{1,0:T(8,128)S(1)} %get-tuple-element.3), channel_id=1, replica_groups=mesh['dp'=32,'tensor'=4] {'dp'}, use_global_device_ids=true, to_apply=%region_6.0 | all-reduce | flops 96 | bytes 768 | tf_op jit(solution)/shard_map/pmax | solution.py:21
  123.0 1.1 fusion.24
  124.1 64.9 %psum.37 = f32[6,16]{1,0:T(8,128)S(1)} all-reduce(f32[6,16]{1,0:T(8,128)S(1)} %fusion.24), channel_id=1, replica_groups=mesh['dp'=32,'tensor'=4] {'dp'}, use_global_device_ids=true, to_apply=%region_8.0 | all-reduce | flops 96 | bytes 768 | tf_op jit(solution)/shard_map/psum | solution.py:26
  189.0 3.9 convolution_divide_fusion
  192.8 121.7 %all-reduce.5 = bf16[6,16,1024]{2,1,0:T(8,128)(2,1)S(1)} all-reduce(f32[6,16,1024]{2,1,0:T(8,128)S(1)} %convolution_divide_fusion), channel_id=1, replica_groups=mesh['dp'=32,'tensor'=4] {'dp'}, use_global_device_ids=true, to_apply=%region_9.0 | all-reduce | flops 98304 | bytes 589824 | tf_op jit(solution)/shard_map/psum | solution.py:27
  314.6 8.8 %all_to_all.33 = bf16[6,16,1024]{2,0,1:T(8,128)(2,1)S(1)} all-to-all(bf16[6,16,1024]{2,0,1:T(8,128)(2,1)S(1)} %copy.20), channel_id=1, replica_groups=mesh['dp'=32,'tensor'=4] {'tensor'}, dimensions={1} | all-to-all | bytes 393216 | tf_op jit(solution)/shard_map/all_to_all | solution.py:34
  323.7 3.2 fusion.6
  326.9 4.9 fusion
  331.8 128.2 %all-reduce.6 = bf16[6,4,4096]{2,1,0:T(4,128)(2,1)S(1)} all-reduce(f32[6,4,4096]{2,1,0:T(4,128)S(1)} %fusion), channel_id=1, replica_groups=mesh['dp'=32,'tensor'=4] {'dp'}, use_global_device_ids=true, to_apply=%region_10.11 | all-reduce | flops 98304 | bytes 589824 | tf_op jit(solution)/shard_map/psum | solution.py:42
  459.9 4.8 copy.24
  464.7 8.1 %reshape.46 = bf16[4,2,12288]{2,1,0:T(2,128)(2,1)} reshape(bf16[4096,4,6]{2,1,0:T(4,128)(2,1)} %bitcast.68) | data formatting | bytes 393216
  472.8 3.5 all-to-all-start.1
  476.3 0.6 log_add_fusion
  476.9 4.3 all-to-all-done.1
  481.3 10.5 %reshape.47 = bf16[4096,4,6]{2,1,0:T(4,128)(2,1)} reshape(bf16[4,2,12288]{2,1,0:T(2,128)(2,1)S(1)} %all-to-all-done.1) | data formatting | bytes 393216
  491.7 6.2 %copy.26 = bf16[6,4,4,1024]{3,2,1,0:T(4,128)(2,1)S(1)} copy(bf16[6,4,4,1024]{0,2,3,1:T(4,128)(2,1)} %bitcast.69) | data formatting | bytes 393216 | tf_op jit(solution)/shard_map/all_to_all | solution.py:43
  498.0 4.5 convolution_convert_fusion
  (10 shorter events, 0.6 us)
Async XLA Ops:
  7.2 0.8 copy-start
  7.2 49.0 %all-reduce.4.cloned.1.call-start = ((), (), s32[]{:S(2)}) async-start(), calls=%async_computation.2 | async-start | bytes 393216 | tf_op jit(solution)/shard_map/psum | solution.py:18
  472.8 8.5 %all-to-all-start.1 = ((bf16[4,2,12288]{2,1,0:T(2,128)(2,1)}), bf16[4,2,12288]{2,1,0:T(2,128)(2,1)S(1)}, u32[]{:S(2)}, u32[]{:S(2)}) async-start(bf16[4,2,12288]{2,1,0:T(2,128)(2,1)} %reshape.46), calls=%async_computation.1 | async-start | bytes 393216 | tf_op jit(solution)/shard_map/all_to_all | solution.py:43
  476.9 21.0 %copy-start.1 = (f32[6,16,512]{2,1,0:T(8,128)S(1)}, f32[6,16,512]{2,1,0:T(8,128)}, u32[]{:S(2)}) copy-start(f32[6,16,512]{2,1,0:T(8,128)} %all-reduce.4.cloned.1.call-done) | copy-start | bytes 589828
Sparse Core Ops, SparseCore 0:
  13.3 42.8 all-reduce.3
where the time goes:
time: 516 us; the launch traced here: 509 us
  blocking collectives  403 us (78%)
  local copies, waits for them, and re-layouts  30.6 us (6%)
  waiting for transfers between devices  28 us (5%)
  matrix products  21.7 us (4%)
  between operations  14.1 us (3%)
  other arithmetic  7.83 us (2%)
    psum x1, blocking collectives, per_device(): slot_out = lax.psum(partial_out, 'dp').astype(jnp.bfloat16)  128 us
    psum x1, blocking collectives, per_device(): lax.psum(partial_value / column_sum[:, :, None], 'dp').astype(jnp.bfloat16)  122 us
    psum x1, blocking collectives, per_device(): column_sum = lax.psum(local_sum, 'dp')  64.9 us
    pmax x1, blocking collectives, per_device(): peaks = lax.pmax(jnp.max(logits, axis=2), 'dp')  64.8 us
    psum x1, waiting for transfers between devices, per_device(): raw_logits, squares = lax.psum((raw_logits, squares), 'tensor')  23.6 us
    unnamed x6, local copies, waits for them, and re-layouts  19.2 us
    psum x1, blocking collectives, per_device(): raw_logits, squares = lax.psum((raw_logits, squares), 'tensor')  15.2 us
  transfers between devices with their start and end apart: 2, of which 2 were waited for; matrix products, arithmetic and copies ran while one was open for 1% of the time, Pallas kernels for 0%

commit v1 on v0

v1 whole, which is shorter than its diff:
```python
import functools

import jax
import jax.numpy as jnp
from jax import lax
from jax.experimental import pallas as pl
from jax.experimental.pallas import tpu as pltpu
from jax.sharding import PartitionSpec as P

GROUPS = 6
SLOTS = 4
EXPERTS = 4
WS = SLOTS * EXPERTS
PAD = 8
LANES = 128
TILES = 8
TOK = 512
WIDTH = TILES * LANES
FULL = 4096
HID = 448
HALF = GROUPS // 2
LROWS = HALF * WS + PAD

epsilon = 1e-05
bf16 = jnp.bfloat16
f32 = jnp.float32
NT = (((1,), (1,)), ((), ()))
VM = pl.BlockSpec(memory_space=pltpu.VMEM)


def params(mib):
    return pltpu.CompilerParams(vmem_limit_bytes=mib << 20)


def logits_kernel(tokens_ref, router_ref, out_ref):
    step = pl.program_id(0)
    tok = tokens_ref[0]
    out_ref[pl.ds(pl.multiple_of(step * WS, WS), WS), :] = lax.dot_general(
        router_ref[...], tok, NT, preferred_element_type=f32
    )
    total = jnp.zeros((TOK, LANES), f32)
    for t in range(TILES):
        part = tok[:, t * LANES:(t + 1) * LANES].astype(f32)
        total += part * part
    row = lax.dot_general(
        jnp.ones((PAD, LANES), f32), total, NT,
        precision=lax.Precision.HIGHEST, preferred_element_type=f32,
    )

    @pl.when(step == 0)
    def _():
        out_ref[HALF * WS:, :] = jnp.zeros((PAD, TOK), f32)

    out_ref[pl.ds(HALF * WS + step, 1), :] = row[0:1]


def partial_logits(tokens, router, half):
    return pl.pallas_call(
        logits_kernel,
        grid=(HALF,),
        in_specs=[
            pl.BlockSpec((1, TOK, WIDTH), lambda g: (half * HALF + g, 0, 0)),
            pl.BlockSpec((WS, WIDTH), lambda g: (0, 0)),
        ],
        out_specs=pl.BlockSpec((LROWS, TOK), lambda g: (0, 0)),
        out_shape=jax.ShapeDtypeStruct((LROWS, TOK), f32),
        compiler_params=params(16),
        name="partial_logits",
    )(tokens, router)


def split3(value):
    high = value.astype(bf16).astype(f32)
    rest = value - high
    mid = rest.astype(bf16).astype(f32)
    return high, mid, rest - mid


def spread_rows(ref, rows, value):
    for n in range(TOK // LANES):
        ref[n, rows, :] = value[:, n * LANES:(n + 1) * LANES]


def dispatch_kernel(*refs):
    parts, (tokens_ref, send_ref, combine_ref, log_ref, wts, cmb, peaks, sums) = refs[:8], refs[8:]
    wts[...] = jnp.zeros_like(wts)
    cmb[...] = jnp.zeros_like(cmb)
    peaks[...] = jnp.zeros_like(peaks)
    sums[...] = jnp.zeros_like(sums)
    for half in range(2):
        a, b, c, d = (ref[...] for ref in parts[half * 4:half * 4 + 4])
        total = (a + b) + (c + d)
        squares = total[HALF * WS:]
        scale = lax.rsqrt(squares * (1.0 / FULL) + epsilon)
        for h in range(HALF):
            g = half * HALF + h
            rows = pl.ds(g, WS, stride=PAD)
            norm = scale[h:h + 1]
            logits = total[h * WS:(h + 1) * WS] * norm
            peak = jnp.max(logits, axis=1, keepdims=True)
            powers = jnp.exp(logits - peak)
            spread_rows(wts, rows, powers * norm)
            peaks[rows, :] = jnp.broadcast_to(peak, (WS, LANES))
            sums[rows, :] = jnp.broadcast_to(jnp.sum(powers, axis=1, keepdims=True), (WS, LANES))
            row_peak = jnp.max(logits, axis=0, keepdims=True)
            row_powers = jnp.exp(logits - row_peak)
            row_sum = jnp.sum(row_powers, axis=0, keepdims=True)
            spread_rows(cmb, rows, row_powers / row_sum)
            log_ref[g:g + 1, :] = row_peak + jnp.log(row_sum)
    combine = jnp.concatenate([cmb[n] for n in range(TOK // LANES)], axis=1)
    combine_ref[...] = jnp.concatenate(
        [combine[(4 * k + s) * PAD:(4 * k + s + 1) * PAD] for s in range(SLOTS) for k in range(EXPERTS)]
    ).astype(bf16)
    weights = jnp.concatenate([wts[n] for n in range(TOK // LANES)], axis=1).astype(bf16)
    group = lax.broadcasted_iota(jnp.int32, (WS * PAD, TOK), 0) % PAD
    acc = jnp.zeros((WS * PAD, WIDTH), f32)
    for g in range(GROUPS):
        mine = jnp.where(group == g, weights, jnp.zeros_like(weights))
        acc += jnp.dot(mine, tokens_ref[g], preferred_element_type=f32)
    lane = lax.broadcasted_iota(jnp.int32, (WS * PAD, LANES), 1)
    member = lax.broadcasted_iota(jnp.int32, (WS * PAD, LANES), 0) % PAD
    meta = jnp.zeros((WS * PAD, LANES), f32)
    for n, value in enumerate(split3(peaks[...]) + split3(sums[...])):
        meta += jnp.where(lane == member + n * PAD, value, 0.0)
    meta = jnp.sum(meta.reshape(WS, PAD, LANES), axis=1, keepdims=True)
    meta = jnp.broadcast_to(meta, (WS, PAD, LANES)).reshape(WS * PAD, LANES)
    for t in range(TILES):
        tile = jnp.where(member == GROUPS, meta, acc[:, t * LANES:(t + 1) * LANES])
        for s in range(SLOTS):
            block = jnp.concatenate(
                [tile[(4 * k + s) * PAD:(4 * k + s + 1) * PAD] for k in range(EXPERTS)]
            )
            send_ref[pl.ds((s * TILES + t) * EXPERTS * PAD, EXPERTS * PAD), :] = block.astype(bf16)


def dispatch(parts, tokens):
    return pl.pallas_call(
        dispatch_kernel,
        in_specs=[VM] * 9,
        out_specs=[VM] * 3,
        out_shape=[
            jax.ShapeDtypeStruct((SLOTS * TILES * EXPERTS * PAD, LANES), bf16),
            jax.ShapeDtypeStruct((WS * PAD, TOK), bf16),
            jax.ShapeDtypeStruct((GROUPS, TOK), f32),
        ],
        scratch_shapes=[
            pltpu.VMEM((TOK // LANES, WS * PAD, LANES), f32),
            pltpu.VMEM((TOK // LANES, WS * PAD, LANES), f32),
            pltpu.VMEM((WS * PAD, LANES), f32),
            pltpu.VMEM((WS * PAD, LANES), f32),
        ],
        compiler_params=params(20),
        name="dispatch",
    )(*parts, tokens)


def merge_kernel(got_ref, out_ref, wide):
    wide[...] = got_ref[...].astype(f32)
    meta = wide[pl.ds(GROUPS, 32, stride=EXPERTS * PAD), :]
    shift = lambda n: pltpu.roll(meta, (LANES - n * PAD) % LANES, 1)
    lane = lax.broadcasted_iota(jnp.int32, (32, LANES), 1)
    peak = (meta + shift(1)) + shift(2)
    local = (shift(3) + shift(4)) + shift(5)
    peak = jnp.where(lane < GROUPS, peak, 0.0)
    factor = jnp.exp(peak - jnp.max(peak, axis=0, keepdims=True))
    total = jnp.sum(factor * local, axis=0, keepdims=True)
    factor = jnp.where(lane < GROUPS, factor / jnp.where(lane[0:1] < GROUPS, total, 1.0), 0.0)
    square = jnp.concatenate([factor, jnp.zeros((LANES - 32, LANES), f32)])
    columns = square.T[0:PAD]
    acc = [jnp.zeros((PAD, LANES), f32) for _ in range(4)]
    for i in range(32):
        by = jnp.broadcast_to(columns[:, i:i + 1], (PAD, LANES))
        for z in range(4):
            row = (i * 4 + z) * PAD
            acc[z] += by * wide[row:row + PAD, :]
    block = jnp.concatenate(acc).astype(bf16)
    for i in range(32):
        out_ref[i] = block


def add_kernel(got_ref, out_ref):
    rows = 4 * PAD
    acc = got_ref[0:rows, :].astype(f32)
    for i in range(1, 32):
        acc += got_ref[i * rows:(i + 1) * rows, :].astype(f32)
    block = acc.astype(bf16)
    for i in range(32):
        out_ref[i] = block


def merge(got):
    return pl.pallas_call(
        merge_kernel,
        in_specs=[VM],
        out_specs=VM,
        out_shape=jax.ShapeDtypeStruct((32, 4 * PAD, LANES), bf16),
        scratch_shapes=[pltpu.VMEM((32 * 4 * PAD, LANES), f32)],
        compiler_params=params(8),
        name="merge",
    )(got)


def add_up(got):
    return pl.pallas_call(
        add_kernel,
        in_specs=[VM],
        out_specs=VM,
        out_shape=jax.ShapeDtypeStruct((32, 4 * PAD, LANES), bf16),
        compiler_params=params(8),
        name="add_up",
    )(got)


def expert_kernel(got_ref, gate_ref, up_ref, down_ref, send_ref, rows):
    for s in range(SLOTS):
        for t in range(TILES):
            block = got_ref[s * TILES + t].astype(f32)
            for z in range(4):
                at = (z * TILES + t) * LANES
                rows[s * PAD:(s + 1) * PAD, at:at + LANES] = block[z * PAD:(z + 1) * PAD]
    slot_in = rows[...].astype(bf16)
    gate = lax.dot_general(slot_in, gate_ref[0], NT, preferred_element_type=f32)
    up = lax.dot_general(slot_in, up_ref[0], NT, preferred_element_type=f32)
    hidden = (gate / (1.0 + jnp.exp(-gate)) * up).astype(bf16)
    out = jnp.dot(hidden, down_ref[0], preferred_element_type=f32)
    for s in range(SLOTS):
        for t in range(TILES):
            block = jnp.concatenate(
                [
                    out[s * PAD:(s + 1) * PAD, (z * TILES + t) * LANES:(z * TILES + t + 1) * LANES]
                    for z in range(4)
                ]
            )
            send_ref[pl.ds((s * TILES + t) * 4 * PAD, 4 * PAD), :] = block.astype(bf16)


def expert(got, w_gate, w_up, w_down):
    return pl.pallas_call(
        expert_kernel,
        in_specs=[VM] * 4,
        out_specs=VM,
        out_shape=jax.ShapeDtypeStruct((SLOTS * TILES * 4 * PAD, LANES), bf16),
        scratch_shapes=[pltpu.VMEM((SLOTS * PAD, FULL), f32)],
        compiler_params=params(24),
        name="expert",
    )(got, w_gate, w_up, w_down)


def mix_kernel(got_ref, combine_ref, out_ref, slots, turned):
    step = pl.program_id(0)

    @pl.when(step == 0)
    def _():
        for s in range(SLOTS):
            for t in range(TILES):
                slots[s * 32:(s + 1) * 32, t * LANES:(t + 1) * LANES] = got_ref[s * TILES + t]
        turned[...] = combine_ref[...].astype(f32).T

    lane = lax.broadcasted_iota(jnp.int32, (TOK, WS * PAD), 1) % PAD
    mine = jnp.where(lane == step, turned[...], 0.0).astype(bf16)
    out_ref[0] = jnp.dot(mine, slots[...], preferred_element_type=f32).astype(bf16)


def mix(got, combine):
    return pl.pallas_call(
        mix_kernel,
        grid=(GROUPS,),
        in_specs=[
            pl.BlockSpec((32, 4 * PAD, LANES), lambda g: (0, 0, 0)),
            pl.BlockSpec((WS * PAD, TOK), lambda g: (0, 0)),
        ],
        out_specs=pl.BlockSpec((1, TOK, WIDTH), lambda g: (g, 0, 0)),
        out_shape=jax.ShapeDtypeStruct((GROUPS, TOK, WIDTH), bf16),
        scratch_shapes=[
            pltpu.VMEM((WS * PAD, WIDTH), bf16),
            pltpu.VMEM((TOK, WS * PAD), f32),
        ],
        compiler_params=params(20),
        name="mix",
    )(got, combine)


def everyone(x):
    x = x.reshape(128, PAD, LANES)
    x = lax.all_to_all(x, ("dp", "tensor"), 0, 0, tiled=True)
    return x.reshape(128 * PAD, LANES)


def per_device(tokens, router, w_gate, w_up, w_down):
    parts = []
    for half in range(2):
        own = partial_logits(tokens, router, half)
        parts.append(own)
        for k in range(1, 4):
            parts.append(lax.ppermute(own, "tensor", [(i, (i + k) % 4) for i in range(4)]))
    send, combine, log_total = dispatch(parts, tokens)
    spread = merge(everyone(send))
    slot_in = lax.all_to_all(spread, "dp", 0, 0, tiled=True)
    outs = expert(slot_in, w_gate, w_up, w_down)
    spread = add_up(everyone(outs))
    slot_out = lax.all_to_all(spread, "dp", 0, 0, tiled=True)
    return (mix(slot_out, combine), log_total)


def solution(mesh):
    in_specs = (
        P(None, "dp", "tensor"),
        P(None, "tensor"),
        P("tensor", "dp", None),
        P("tensor", "dp", None),
        P("tensor", "dp", None),
    )
    out_specs = (P(None, "dp", "tensor"), P(None, "dp"))
    return jax.shard_map(
        per_device, mesh=mesh, in_specs=in_specs, out_specs=out_specs, check_vma=False
    )
```

time: 516 us -> 93.8 us (0.18); the launches traced: 509 us -> 93.5 us
  blocking collectives: 403 us -> 60.6 us
  local copies, waits for them, and re-layouts: 30.6 us -> 3.57 us
  waiting for transfers between devices: 28 us -> 6.09 us
  matrix products: 21.7 us -> 0 us
  between operations: 14.1 us -> 0.68 us
  Pallas kernels: 0 us -> 13.4 us
  other arithmetic: 7.83 us -> 0 us
  starting transfers between devices: 3.58 us -> 9.13 us
    psum x4 -> x0, blocking collectives: 330 us -> none  [the longest x1 128 us: per_device(): slot_out = lax.psum(partial_out, 'dp').astype(jnp.bfloat16)]
    pmax x1 -> x0, blocking collectives: 64.8 us -> none  [per_device(): peaks = lax.pmax(jnp.max(logits, axis=2), 'dp')]
    all_to_all x1 -> x4, blocking collectives: 8.75 us -> 60.6 us  [the longest x2 35.2 us: everyone(): x = lax.all_to_all(x, ('dp', 'tensor'), 0, 0, tiled=True)]
    psum x1 -> x0, waiting for transfers between devices: 23.6 us -> none  [per_device(): raw_logits, squares = lax.psum((raw_logits, squares), 'tensor')]
    dot_general x5 -> x0, matrix products: 21.7 us -> none  [the longest x1 5.2 us: per_device(): jnp.einsum('sd,gtd->gst', router, tokens, preferred_element_type=jnp.floa...]
    unnamed x6 -> x14, local copies, waits for them, and re-layouts: 19.2 us -> 3.57 us
    pallas_call x0 -> x7, Pallas kernels: none -> 13.4 us  [the longest x1 4.7 us: mix(): pl.pallas_call(mix_kernel, grid=(GROUPS,), in_specs=[pl.BlockSpec((32, 4...]
    ppermute x0 -> x6, starting transfers between devices: none -> 9.13 us  [per_device(): lax.ppermute(own, 'tensor', [(i, (i + k) % 4) for i in range(4)])]
  transfers between devices with their start and end apart: 2 -> 6, of which waited for: 2 -> 3; matrix products, arithmetic and copies ran while one was open for 1% -> 0% of each run, Pallas kernels for 0% -> 2%
where the time goes in v1:
time: 93.8 us; the launch traced here: 93.5 us
  blocking collectives  60.6 us (65%)
  Pallas kernels  13.4 us (14%)
  starting transfers between devices  9.13 us (10%)
  waiting for transfers between devices  6.09 us (6%)
  local copies, waits for them, and re-layouts  3.57 us (4%)
    all_to_all x2, blocking collectives, everyone(): x = lax.all_to_all(x, ('dp', 'tensor'), 0, 0, tiled=True)  35.2 us
    all_to_all x1, blocking collectives, per_device(): slot_in = lax.all_to_all(spread, 'dp', 0, 0, tiled=True)  12.7 us
    all_to_all x1, blocking collectives, per_device(): slot_out = lax.all_to_all(spread, 'dp', 0, 0, tiled=True)  12.7 us
    ppermute x6, starting transfers between devices, per_device(): lax.ppermute(own, 'tensor', [(i, (i + k) % 4) for i in range(4)])  9.13 us
    ppermute x6, waiting for transfers between devices, per_device(): lax.ppermute(own, 'tensor', [(i, (i + k) % 4) for i in range(4)])  6.09 us
    pallas_call x1, Pallas kernels, mix(): pl.pallas_call(mix_kernel, grid=(GROUPS,), in_specs=[pl.BlockSpec((32, 4...  4.7 us
    pallas_call x2, Pallas kernels, partial_logits(): pl.pallas_call(logits_kernel, grid=(HALF,), in_specs=[pl.BlockSpec((1, TO...  3.66 us
    unnamed x14, local copies, waits for them, and re-layouts  3.57 us
  transfers between devices with their start and end apart: 6, of which 3 were waited for; matrix products, arithmetic and copies ran while one was open for 0% of the time, Pallas kernels for 2%

profile of v1, /device:TPU:1, one launch (start us, length us, event | category | flops | bytes accessed | tf_op | source)
XLA Modules:
  0.0 93.5 jit_solution(5622497463421970227)
XLA Ops:
  0.6 0.0 copy-start
  0.6 2.8 %copy-done = bf16[6,512,1024]{2,1,0:T(8,128)(2,1)S(1)} copy-done((bf16[6,512,1024]{2,1,0:T(8,128)(2,1)S(1)}, bf16[6,512,1024]{2,1,0:T(8,128)(2,1)}, u32[]{:S(2)}) %copy-start) | copy-done | bytes 6291480
  3.4 0.8 copy-done.5
  4.2 1.8 %partial_logits.2.refs_0_ = f32[56,512]{1,0:T(8,128)S(1)} custom-call(bf16[6,512,1024]{2,1,0:T(8,128)(2,1)S(1)} %copy-done, bf16[16,1024]{1,0:T(8,128)(2,1)S(1)} %copy-done.5), custom_call_target="tpu_custom_call" | custom-call | tf_op jit(solution)/shard_map/partial_logits/pallas_call | solution.py:58
  6.0 4.6 %collective-permute-start.2 = (f32[56,512]{1,0:T(8,128)S(1)}, f32[56,512]{1,0:T(8,128)S(1)}, u32[]{:S(2)}, u32[]{:S(2)}) collective-permute-start(f32[56,512]{1,0:T(8,128)S(1)} %partial_logits.2.refs_0_), channel_id=1, source_target_pairs={{0,3},{1,0},{2,1},{3,2},{4,7},{5,4},{6,5},{7,6},{8,11},{9,8},{10,9... | collective-permute-start | bytes 344072 | tf_op jit(solution)/shard_map/ppermute | solution.py:295
  10.6 0.7 collective-permute-start
  11.3 1.8 %partial_logits.3.refs_4_ = f32[56,512]{1,0:T(8,128)S(1)} custom-call(bf16[6,512,1024]{2,1,0:T(8,128)(2,1)S(1)} %copy-done, bf16[16,1024]{1,0:T(8,128)(2,1)S(1)} %copy-done.6), custom_call_target="tpu_custom_call" | custom-call | tf_op jit(solution)/shard_map/partial_logits/pallas_call | solution.py:58
  13.2 0.0 copy-start.3
  13.2 2.0 %collective-permute-start.5 = (f32[56,512]{1,0:T(8,128)S(1)}, f32[56,512]{1,0:T(8,128)S(1)}, u32[]{:S(2)}, u32[]{:S(2)}) collective-permute-start(f32[56,512]{1,0:T(8,128)S(1)} %partial_logits.3.refs_4_), channel_id=1, source_target_pairs={{0,3},{1,0},{2,1},{3,2},{4,7},{5,4},{6,5},{7,6},{8,11},{9,8},{10,9... | collective-permute-start | bytes 344072 | tf_op jit(solution)/shard_map/ppermute | solution.py:295
  15.2 1.8 %collective-permute-start.4 = (f32[56,512]{1,0:T(8,128)S(1)}, f32[56,512]{1,0:T(8,128)S(1)}, u32[]{:S(2)}, u32[]{:S(2)}) collective-permute-start(f32[56,512]{1,0:T(8,128)S(1)} %partial_logits.3.refs_4_), channel_id=1, source_target_pairs={{0,2},{1,3},{2,0},{3,1},{4,6},{5,7},{6,4},{7,5},{8,10},{9,11},{10,... | collective-permute-start | bytes 344072 | tf_op jit(solution)/shard_map/ppermute | solution.py:295
  17.0 0.0 collective-permute-done.2.refs_3_
  17.0 0.0 collective-permute-start.3
  17.0 2.0 %collective-permute-done.refs_1_ = f32[56,512]{1,0:T(8,128)S(1)} collective-permute-done((f32[56,512]{1,0:T(8,128)S(1)}, f32[56,512]{1,0:T(8,128)S(1)}, u32[]{:S(2)}, u32[]{:S(2)}) %collective-permute-start) | collective-permute-done | bytes 114720 | tf_op jit(solution)/shard_map/ppermute | solution.py:295
  19.0 1.7 %collective-permute-done.4.refs_6_ = f32[56,512]{1,0:T(8,128)S(1)} collective-permute-done((f32[56,512]{1,0:T(8,128)S(1)}, f32[56,512]{1,0:T(8,128)S(1)}, u32[]{:S(2)}, u32[]{:S(2)}) %collective-permute-start.4) | collective-permute-done | bytes 114720 | tf_op jit(solution)/shard_map/ppermute | solution.py:295
  20.8 2.3 %collective-permute-done.3.refs_5_ = f32[56,512]{1,0:T(8,128)S(1)} collective-permute-done((f32[56,512]{1,0:T(8,128)S(1)}, f32[56,512]{1,0:T(8,128)S(1)}, u32[]{:S(2)}, u32[]{:S(2)}) %collective-permute-start.3) | collective-permute-done | bytes 114720 | tf_op jit(solution)/shard_map/ppermute | solution.py:295
  23.1 1.8 %dispatch.1 = (bf16[1024,128]{1,0:T(8,128)(2,1)S(1)}, bf16[128,512]{1,0:T(8,128)(2,1)S(1)}, f32[6,512]{1,0:T(8,128)}) custom-call(f32[56,512]{1,0:T(8,128)S(1)} %partial_logits.2.refs_0_, f32[56,512]{1,0:T(8,128)S(1)} %collective-permute-done.refs_1_, f32[56,512]{1,0:T(8,128)S(1)} %collective-permute-done.1.refs_2_, ...), custom_call_target="tpu_custom_call" | custom-call | tf_op jit(solution)/shard_map/dispatch/pallas_call | solution.py:137
  24.9 20.3 %all_to_all.20 = bf16[128,8,128]{2,1,0:T(8,128)(2,1)S(1)} all-to-all(bf16[128,8,128]{2,1,0:T(8,128)(2,1)S(1)} %bitcast.7), channel_id=1, replica_groups=mesh['dp'=32,'tensor'=4] {'dp','tensor'}, dimensions={0} | all-to-all | bytes 524288 | tf_op jit(solution)/shard_map/all_to_all | solution.py:285
  45.2 0.4 merge.1
  45.5 12.7 %all_to_all.21.got_ref = bf16[32,32,128]{2,1,0:T(8,128)(2,1)S(1)} all-to-all(bf16[32,32,128]{2,1,0:T(8,128)(2,1)S(1)} %merge.1), channel_id=1, replica_groups=mesh['dp'=32,'tensor'=4] {'dp'}, dimensions={0} | all-to-all | bytes 524288 | tf_op jit(solution)/shard_map/all_to_all | solution.py:298
  58.2 2.8 %expert.1 = bf16[1024,128]{1,0:T(8,128)(2,1)S(1)} custom-call(bf16[32,32,128]{2,1,0:T(8,128)(2,1)S(1)} %all_to_all.21.got_ref, bf16[1,448,4096]{2,1,0:T(8,128)(2,1)S(1)} %copy-done.2, bf16[1,448,4096]{2,1,0:T(8,128)(2,1)S(1)} %copy-done.3, bf16[1,448,4096]{2,1,0:T(8,128)(2,1)S(1)} %copy-done.4), custom_call_target="tpu_custom_call" | custom-call | tf_op jit(solution)/shard_map/expert/pallas_call | solution.py:238
  61.1 14.9 %all_to_all.22 = bf16[128,8,128]{2,1,0:T(8,128)(2,1)S(1)} all-to-all(bf16[128,8,128]{2,1,0:T(8,128)(2,1)S(1)} %bitcast.4), channel_id=1, replica_groups=mesh['dp'=32,'tensor'=4] {'dp','tensor'}, dimensions={0} | all-to-all | bytes 524288 | tf_op jit(solution)/shard_map/all_to_all | solution.py:285
  76.0 0.1 add_up.1
  76.1 12.7 %all_to_all.23.got_ref = bf16[32,32,128]{2,1,0:T(8,128)(2,1)S(1)} all-to-all(bf16[32,32,128]{2,1,0:T(8,128)(2,1)S(1)} %add_up.1), channel_id=1, replica_groups=mesh['dp'=32,'tensor'=4] {'dp'}, dimensions={0} | all-to-all | bytes 524288 | tf_op jit(solution)/shard_map/all_to_all | solution.py:301
  88.8 4.7 %mix.1 = bf16[6,512,1024]{2,1,0:T(8,128)(2,1)} custom-call(bf16[32,32,128]{2,1,0:T(8,128)(2,1)S(1)} %all_to_all.23.got_ref, bf16[128,512]{1,0:T(8,128)(2,1)S(1)} %get-tuple-element.6.combine_ref), custom_call_target="tpu_custom_call" | custom-call | tf_op jit(solution)/shard_map/mix/pallas_call | solution.py:265
  (13 shorter events, 0.0 us)
Async XLA Ops:
  0.6 2.8 %copy-start = (bf16[6,512,1024]{2,1,0:T(8,128)(2,1)S(1)}, bf16[6,512,1024]{2,1,0:T(8,128)(2,1)}, u32[]{:S(2)}) copy-start(bf16[6,512,1024]{2,1,0:T(8,128)(2,1)} %refs_8_.1) | copy-start | bytes 18874372
  3.4 0.8 copy-start.5
  4.2 7.2 %copy-start.6 = (bf16[16,1024]{1,0:T(8,128)(2,1)S(1)}, bf16[16,1024]{1,0:T(8,128)(2,1)}, u32[]{:S(2)}) copy-start(bf16[16,1024]{1,0:T(8,128)(2,1)} %router_ref.3) | copy-start | bytes 98308
  4.2 54.1 %copy-start.4 = (bf16[1,448,4096]{2,1,0:T(8,128)(2,1)S(1)}, bf16[1,448,4096]{2,1,0:T(8,128)(2,1)}, u32[]{:S(2)}) copy-start(bf16[1,448,4096]{2,1,0:T(8,128)(2,1)} %down_ref.1) | copy-start | bytes 11010052
  6.0 17.1 %copy-start.1 = (bf16[6,512,1024]{2,1,0:T(8,128)(2,1)S(1)}, bf16[6,512,1024]{2,1,0:T(8,128)(2,1)}, u32[]{:S(2)}) copy-start(bf16[6,512,1024]{2,1,0:T(8,128)(2,1)} %refs_8_.1) | copy-start | bytes 18874372
  6.0 11.0 %collective-permute-start.2 = (f32[56,512]{1,0:T(8,128)S(1)}, f32[56,512]{1,0:T(8,128)S(1)}, u32[]{:S(2)}, u32[]{:S(2)}) collective-permute-start(f32[56,512]{1,0:T(8,128)S(1)} %partial_logits.2.refs_0_), channel_id=1, source_target_pairs={{0,3},{1,0},{2,1},{3,2},{4,7},{5,4},{6,5},{7,6},{8,11},{9,8},{10,9... | collective-permute-start | bytes 344072 | tf_op jit(solution)/shard_map/ppermute | solution.py:295
  10.6 6.4 %collective-permute-start.1 = (f32[56,512]{1,0:T(8,128)S(1)}, f32[56,512]{1,0:T(8,128)S(1)}, u32[]{:S(2)}, u32[]{:S(2)}) collective-permute-start(f32[56,512]{1,0:T(8,128)S(1)} %partial_logits.2.refs_0_), channel_id=1, source_target_pairs={{0,2},{1,3},{2,0},{3,1},{4,6},{5,7},{6,4},{7,5},{8,10},{9,11},{10,... | collective-permute-start | bytes 344072 | tf_op jit(solution)/shard_map/ppermute | solution.py:295
  10.6 8.4 %collective-permute-start = (f32[56,512]{1,0:T(8,128)S(1)}, f32[56,512]{1,0:T(8,128)S(1)}, u32[]{:S(2)}, u32[]{:S(2)}) collective-permute-start(f32[56,512]{1,0:T(8,128)S(1)} %partial_logits.2.refs_0_), channel_id=1, source_target_pairs={{0,1},{1,2},{2,3},{3,0},{4,5},{5,6},{6,7},{7,4},{8,9},{9,10},{10,1... | collective-permute-start | bytes 344072 | tf_op jit(solution)/shard_map/ppermute | solution.py:295
  13.2 45.1 %copy-start.2 = (bf16[1,448,4096]{2,1,0:T(8,128)(2,1)S(1)}, bf16[1,448,4096]{2,1,0:T(8,128)(2,1)}, u32[]{:S(2)}) copy-start(bf16[1,448,4096]{2,1,0:T(8,128)(2,1)} %gate_ref.1) | copy-start | bytes 11010052
  13.2 45.1 %copy-start.3 = (bf16[1,448,4096]{2,1,0:T(8,128)(2,1)S(1)}, bf16[1,448,4096]{2,1,0:T(8,128)(2,1)}, u32[]{:S(2)}) copy-start(bf16[1,448,4096]{2,1,0:T(8,128)(2,1)} %up_ref.1) | copy-start | bytes 11010052
  13.2 5.8 %collective-permute-start.5 = (f32[56,512]{1,0:T(8,128)S(1)}, f32[56,512]{1,0:T(8,128)S(1)}, u32[]{:S(2)}, u32[]{:S(2)}) collective-permute-start(f32[56,512]{1,0:T(8,128)S(1)} %partial_logits.3.refs_4_), channel_id=1, source_target_pairs={{0,3},{1,0},{2,1},{3,2},{4,7},{5,4},{6,5},{7,6},{8,11},{9,8},{10,9... | collective-permute-start | bytes 344072 | tf_op jit(solution)/shard_map/ppermute | solution.py:295
  15.2 5.5 %collective-permute-start.4 = (f32[56,512]{1,0:T(8,128)S(1)}, f32[56,512]{1,0:T(8,128)S(1)}, u32[]{:S(2)}, u32[]{:S(2)}) collective-permute-start(f32[56,512]{1,0:T(8,128)S(1)} %partial_logits.3.refs_4_), channel_id=1, source_target_pairs={{0,2},{1,3},{2,0},{3,1},{4,6},{5,7},{6,4},{7,5},{8,10},{9,11},{10,... | collective-permute-start | bytes 344072 | tf_op jit(solution)/shard_map/ppermute | solution.py:295
  17.0 6.1 %collective-permute-start.3 = (f32[56,512]{1,0:T(8,128)S(1)}, f32[56,512]{1,0:T(8,128)S(1)}, u32[]{:S(2)}, u32[]{:S(2)}) collective-permute-start(f32[56,512]{1,0:T(8,128)S(1)} %partial_logits.3.refs_4_), channel_id=1, source_target_pairs={{0,1},{1,2},{2,3},{3,0},{4,5},{5,6},{6,7},{7,4},{8,9},{9,10},{10,1... | collective-permute-start | bytes 344072 | tf_op jit(solution)/shard_map/ppermute | solution.py:295

commit v2 on v1

--- a/solution.py
+++ b/solution.py
@@ -21,50 +21,59 @@
 HALF = GROUPS // 2
 LROWS = HALF * WS + PAD
 
+CHUNK = 256
+
 epsilon = 1e-05
 bf16 = jnp.bfloat16
 f32 = jnp.float32
 NT = (((1,), (1,)), ((), ()))
 VM = pl.BlockSpec(memory_space=pltpu.VMEM)
+HBM = pl.BlockSpec(memory_space=pltpu.HBM)
 
 
 def params(mib):
     return pltpu.CompilerParams(vmem_limit_bytes=mib << 20)
 
 
-def logits_kernel(tokens_ref, router_ref, out_ref):
-    step = pl.program_id(0)
-    tok = tokens_ref[0]
-    out_ref[pl.ds(pl.multiple_of(step * WS, WS), WS), :] = lax.dot_general(
-        router_ref[...], tok, NT, preferred_element_type=f32
-    )
-    total = jnp.zeros((TOK, LANES), f32)
-    for t in range(TILES):
-        part = tok[:, t * LANES:(t + 1) * LANES].astype(f32)
-        total += part * part
-    row = lax.dot_general(
-        jnp.ones((PAD, LANES), f32), total, NT,
-        precision=lax.Precision.HIGHEST, preferred_element_type=f32,
-    )
-
-    @pl.when(step == 0)
-    def _():
-        out_ref[HALF * WS:, :] = jnp.zeros((PAD, TOK), f32)
-
-    out_ref[pl.ds(HALF * WS + step, 1), :] = row[0:1]
-
-
-def partial_logits(tokens, router, half):
+def logits_kernel(tokens_ref, router_ref, first_ref, second_ref, held_a, held_b, router, arrived):
+    held = [(held_a, held_b)[g // HALF].at[g % HALF] for g in range(GROUPS)]
+    fetch = pltpu.make_async_copy(router_ref, router, arrived.at[GROUPS])
+    fetch.start()
+    copies = [
+        pltpu.make_async_copy(tokens_ref.at[g], held[g], arrived.at[g]) for g in range(GROUPS)
+    ]
+    for copy in copies:
+        copy.start()
+    fetch.wait()
+    for g in range(GROUPS):
+        out_ref, h = (first_ref, second_ref)[g // HALF], g % HALF
+        if h == 0:
+            out_ref[HALF * WS:, :] = jnp.zeros((PAD, TOK), f32)
+        copies[g].wait()
+        tok = held[g][...]
+        out_ref[h * WS:(h + 1) * WS, :] = lax.dot_general(
+            router[...], tok, NT, preferred_element_type=f32
+        )
+        total = jnp.zeros((TOK, LANES), f32)
+        for t in range(TILES):
+            part = tok[:, t * LANES:(t + 1) * LANES].astype(f32)
+            total += part * part
+        out_ref[HALF * WS + h:HALF * WS + h + 1, :] = jnp.sum(total.T, axis=0, keepdims=True)
+
+
+def partial_logits(tokens, router):
+    logits = jax.ShapeDtypeStruct((LROWS, TOK), f32)
+    held = jax.ShapeDtypeStruct((HALF, TOK, WIDTH), tokens.dtype)
     return pl.pallas_call(
         logits_kernel,
-        grid=(HALF,),
-        in_specs=[
-            pl.BlockSpec((1, TOK, WIDTH), lambda g: (half * HALF + g, 0, 0)),
-            pl.BlockSpec((WS, WIDTH), lambda g: (0, 0)),
+        in_specs=[HBM, HBM],
+        out_specs=[VM] * 4,
+        out_shape=[logits, logits, held, held],
+        scratch_shapes=[
+            pltpu.VMEM(router.shape, router.dtype),
+            pltpu.SemaphoreType.DMA((GROUPS + 1,)),
         ],
-        out_specs=pl.BlockSpec((LROWS, TOK), lambda g: (0, 0)),
-        out_shape=jax.ShapeDtypeStruct((LROWS, TOK), f32),
-        compiler_params=params(16),
+        compiler_params=params(46),
         name="partial_logits",
     )(tokens, router)
 
@@ -82,31 +91,28 @@
 
 
 def dispatch_kernel(*refs):
-    parts, (tokens_ref, send_ref, combine_ref, log_ref, wts, cmb, peaks, sums) = refs[:8], refs[8:]
+    parts, (held_a, held_b, send_ref, combine_ref, log_ref, wts, cmb, peaks, sums) = refs[:4], refs[4:]
     wts[...] = jnp.zeros_like(wts)
     cmb[...] = jnp.zeros_like(cmb)
     peaks[...] = jnp.zeros_like(peaks)
     sums[...] = jnp.zeros_like(sums)
-    for half in range(2):
-        a, b, c, d = (ref[...] for ref in parts[half * 4:half * 4 + 4])
-        total = (a + b) + (c + d)
-        squares = total[HALF * WS:]
-        scale = lax.rsqrt(squares * (1.0 / FULL) + epsilon)
-        for h in range(HALF):
-            g = half * HALF + h
-            rows = pl.ds(g, WS, stride=PAD)
-            norm = scale[h:h + 1]
-            logits = total[h * WS:(h + 1) * WS] * norm
-            peak = jnp.max(logits, axis=1, keepdims=True)
-            powers = jnp.exp(logits - peak)
-            spread_rows(wts, rows, powers * norm)
-            peaks[rows, :] = jnp.broadcast_to(peak, (WS, LANES))
-            sums[rows, :] = jnp.broadcast_to(jnp.sum(powers, axis=1, keepdims=True), (WS, LANES))
-            row_peak = jnp.max(logits, axis=0, keepdims=True)
-            row_powers = jnp.exp(logits - row_peak)
-            row_sum = jnp.sum(row_powers, axis=0, keepdims=True)
-            spread_rows(cmb, rows, row_powers / row_sum)
-            log_ref[g:g + 1, :] = row_peak + jnp.log(row_sum)
+    totals = [parts[0][...] + parts[1][...], parts[2][...] + parts[3][...]]
+    scales = [lax.rsqrt(total[HALF * WS:] * (1.0 / FULL) + epsilon) for total in totals]
+    for g in range(GROUPS):
+        half, h = divmod(g, HALF)
+        rows = pl.ds(g, WS, stride=PAD)
+        norm = scales[half][h:h + 1]
+        logits = totals[half][h * WS:(h + 1) * WS] * norm
+        peak = jnp.max(logits, axis=1, keepdims=True)
+        powers = jnp.exp(logits - peak)
+        spread_rows(wts, rows, powers * norm)
+        peaks[rows, :] = jnp.broadcast_to(peak, (WS, LANES))
+        sums[rows, :] = jnp.broadcast_to(jnp.sum(powers, axis=1, keepdims=True), (WS, LANES))
+        row_peak = jnp.max(logits, axis=0, keepdims=True)
+        row_powers = jnp.exp(logits - row_peak)
+        row_sum = jnp.sum(row_powers, axis=0, keepdims=True)
+        spread_rows(cmb, rows, row_powers / row_sum)
+        log_ref[g:g + 1, :] = row_peak + jnp.log(row_sum)
     combine = jnp.concatenate([cmb[n] for n in range(TOK // LANES)], axis=1)
     combine_ref[...] = jnp.concatenate(
         [combine[(4 * k + s) * PAD:(4 * k + s + 1) * PAD] for s in range(SLOTS) for k in range(EXPERTS)]
@@ -116,7 +122,8 @@
     acc = jnp.zeros((WS * PAD, WIDTH), f32)
     for g in range(GROUPS):
         mine = jnp.where(group == g, weights, jnp.zeros_like(weights))
-        acc += jnp.dot(mine, tokens_ref[g], preferred_element_type=f32)
+        held = (held_a, held_b)[g // HALF]
+        acc += jnp.dot(mine, held[g % HALF], preferred_element_type=f32)
     lane = lax.broadcasted_iota(jnp.int32, (WS * PAD, LANES), 1)
     member = lax.broadcasted_iota(jnp.int32, (WS * PAD, LANES), 0) % PAD
     meta = jnp.zeros((WS * PAD, LANES), f32)
@@ -133,10 +140,10 @@
             send_ref[pl.ds((s * TILES + t) * EXPERTS * PAD, EXPERTS * PAD), :] = block.astype(bf16)
 
 
-def dispatch(parts, tokens):
+def dispatch(parts, held):
     return pl.pallas_call(
         dispatch_kernel,
-        in_specs=[VM] * 9,
+        in_specs=[VM] * 6,
         out_specs=[VM] * 3,
         out_shape=[
             jax.ShapeDtypeStruct((SLOTS * TILES * EXPERTS * PAD, LANES), bf16),
@@ -151,7 +158,7 @@
         ],
         compiler_params=params(20),
         name="dispatch",
-    )(*parts, tokens)
+    )(*parts, *held)
 
 
 def merge_kernel(got_ref, out_ref, wide):
@@ -246,36 +253,40 @@
     )(got, w_gate, w_up, w_down)
 
 
-def mix_kernel(got_ref, combine_ref, out_ref, slots, turned):
-    step = pl.program_id(0)
-
-    @pl.when(step == 0)
-    def _():
-        for s in range(SLOTS):
-            for t in range(TILES):
-                slots[s * 32:(s + 1) * 32, t * LANES:(t + 1) * LANES] = got_ref[s * TILES + t]
-        turned[...] = combine_ref[...].astype(f32).T
-
-    lane = lax.broadcasted_iota(jnp.int32, (TOK, WS * PAD), 1) % PAD
-    mine = jnp.where(lane == step, turned[...], 0.0).astype(bf16)
-    out_ref[0] = jnp.dot(mine, slots[...], preferred_element_type=f32).astype(bf16)
+def mix_kernel(got_ref, combine_ref, out_ref, slots, turned, block, left):
+    for s in range(SLOTS):
+        for t in range(TILES):
+            slots[s * 32:(s + 1) * 32, t * LANES:(t + 1) * LANES] = got_ref[s * TILES + t]
+    turned[...] = combine_ref[...].astype(f32).T
+    lane = lax.broadcasted_iota(jnp.int32, (CHUNK, WS * PAD), 1) % PAD
+    copies = []
+    for g in range(GROUPS):
+        for c in range(TOK // CHUNK):
+            rows = pl.ds(c * CHUNK, CHUNK)
+            mine = jnp.where(lane == g, turned[rows, :], 0.0).astype(bf16)
+            block[g, rows, :] = jnp.dot(mine, slots[...], preferred_element_type=f32).astype(bf16)
+            copy = pltpu.make_async_copy(
+                block.at[g, rows], out_ref.at[g, rows], left.at[len(copies)]
+            )
+            copy.start()
+            copies.append(copy)
+    for copy in copies:
+        copy.wait()
 
 
 def mix(got, combine):
     return pl.pallas_call(
         mix_kernel,
-        grid=(GROUPS,),
-        in_specs=[
-            pl.BlockSpec((32, 4 * PAD, LANES), lambda g: (0, 0, 0)),
-            pl.BlockSpec((WS * PAD, TOK), lambda g: (0, 0)),
-        ],
-        out_specs=pl.BlockSpec((1, TOK, WIDTH), lambda g: (g, 0, 0)),
+        in_specs=[VM, VM],
+        out_specs=HBM,
         out_shape=jax.ShapeDtypeStruct((GROUPS, TOK, WIDTH), bf16),
         scratch_shapes=[
             pltpu.VMEM((WS * PAD, WIDTH), bf16),
             pltpu.VMEM((TOK, WS * PAD), f32),
+            pltpu.VMEM((GROUPS, TOK, WIDTH), bf16),
+            pltpu.SemaphoreType.DMA((GROUPS * TOK // CHUNK,)),
         ],
-        compiler_params=params(20),
+        compiler_params=params(24),
         name="mix",
     )(got, combine)
 
@@ -287,13 +298,13 @@
 
 
 def per_device(tokens, router, w_gate, w_up, w_down):
-    parts = []
-    for half in range(2):
-        own = partial_logits(tokens, router, half)
-        parts.append(own)
-        for k in range(1, 4):
-            parts.append(lax.ppermute(own, "tensor", [(i, (i + k) % 4) for i in range(4)]))
-    send, combine, log_total = dispatch(parts, tokens)
+    first, second, held_a, held_b = partial_logits(tokens, router)
+    near = lambda x: lax.ppermute(x, "tensor", [(i, i ^ 1) for i in range(4)])
+    far = lambda x: lax.ppermute(x, "tensor", [(i, i ^ 3) for i in range(4)])
+    first = first + near(first)
+    second = second + far(second)
+    parts = [first, far(first), second, near(second)]
+    send, combine, log_total = dispatch(parts, (held_a, held_b))
     spread = merge(everyone(send))
     slot_in = lax.all_to_all(spread, "dp", 0, 0, tiled=True)
     outs = expert(slot_in, w_gate, w_up, w_down)

time: 93.8 us -> 87.8 us (0.936)
  local copies, waits for them, and re-layouts: 3.57 us -> 0.76 us
  waiting for transfers between devices: 6.09 us -> 4.53 us
  Pallas kernels: 13.4 us -> 12 us
    unnamed x14 -> x8, local copies, waits for them, and re-layouts: 3.57 us -> 0.76 us
    ppermute x6 -> x4, waiting for transfers between devices: 6.09 us -> 4.53 us  [the longest x2 2.47 us: per_device(): near = lambda x: lax.ppermute(x, 'tensor', [(i, i ^ 1) for i in range(4)])]
    pallas_call x4 -> x3, Pallas kernels: 10.1 us -> 8.76 us  [the longest x1 3.89 us: partial_logits(): pl.pallas_call(logits_kernel, in_specs=[HBM, HBM], out_specs=[VM] * 4, ou...]
    ppermute x6 -> x4, starting transfers between devices: 9.13 us -> 8.24 us  [the longest x2 5.61 us: per_device(): far = lambda x: lax.ppermute(x, 'tensor', [(i, i ^ 3) for i in range(4)])]
  transfers between devices with their start and end apart: 6 -> 4, of which waited for: 3 -> 3; matrix products, arithmetic and copies ran while one was open for 0% -> 0% of each run, Pallas kernels for 2% -> 0%
where the time goes in v2:
time: 87.8 us; the launch traced here: 87.5 us
  blocking collectives  61.3 us (70%)
  Pallas kernels  12 us (14%)
  starting transfers between devices  8.24 us (9%)
  waiting for transfers between devices  4.53 us (5%)
    all_to_all x2, blocking collectives, everyone(): x = lax.all_to_all(x, ('dp', 'tensor'), 0, 0, tiled=True)  35.9 us
    all_to_all x1, blocking collectives, per_device(): slot_in = lax.all_to_all(spread, 'dp', 0, 0, tiled=True)  12.7 us
    all_to_all x1, blocking collectives, per_device(): slot_out = lax.all_to_all(spread, 'dp', 0, 0, tiled=True)  12.7 us
    ppermute x2, starting transfers between devices, per_device(): far = lambda x: lax.ppermute(x, 'tensor', [(i, i ^ 3) for i in range(4)])  5.61 us
    pallas_call x1, Pallas kernels, partial_logits(): pl.pallas_call(logits_kernel, in_specs=[HBM, HBM], out_specs=[VM] * 4, ou...  3.89 us
    pallas_call x1, Pallas kernels, mix(): pl.pallas_call(mix_kernel, in_specs=[VM, VM], out_specs=HBM, out_shape=ja...  3.1 us
    pallas_call x1, Pallas kernels, expert(): pl.pallas_call(expert_kernel, in_specs=[VM] * 4, out_specs=VM, out_shape=...  2.83 us
    ppermute x2, starting transfers between devices, per_device(): near = lambda x: lax.ppermute(x, 'tensor', [(i, i ^ 1) for i in range(4)])  2.63 us
  transfers between devices with their start and end apart: 4, of which 3 were waited for; matrix products, arithmetic and copies ran while one was open for 0% of the time, Pallas kernels for 0%

profile of v2, /device:TPU:1, one launch (start us, length us, event | category | flops | bytes accessed | tf_op | source)
XLA Modules:
  0.0 87.5 jit_solution(7754700264648156925)
XLA Ops:
  0.6 0.0 copy-start.3
  0.6 0.7 copy-done.3
  1.4 0.0 copy-start.2
  1.4 3.9 %partial_logits.1 = (f32[56,512]{1,0:T(8,128)S(1)}, f32[56,512]{1,0:T(8,128)S(1)}, bf16[3,512,1024]{2,1,0:T(8,128)(2,1)S(1)}, bf16[3,512,1024]{2,1,0:T(8,128)(2,1)S(1)}) custom-call(bf16[6,512,1024]{2,1,0:T(8,128)(2,1)} %tokens_ref.1, bf16[16,1024]{1,0:T(8,128)(2,1)S(1)} %copy-done.3), custom_call_target="tpu_custom_call" | custom-call | tf_op jit(solution)/shard_map/partial_logits/pallas_call | solution.py:67
  5.3 2.5 %collective-permute-start = (f32[56,512]{1,0:T(8,128)S(1)}, f32[56,512]{1,0:T(8,128)S(1)}, u32[]{:S(2)}, u32[]{:S(2)}) collective-permute-start(f32[56,512]{1,0:T(8,128)S(1)} %get-tuple-element.9), channel_id=1, source_target_pairs={{0,1},{1,0},{2,3},{3,2},{4,5},{5,4},{6,7},{7,6},{8,9},{9,8},{10,11... | collective-permute-start | bytes 344072 | tf_op jit(solution)/shard_map/ppermute | solution.py:302
  7.8 2.2 %collective-permute-start.2 = (f32[56,512]{1,0:T(8,128)S(1)}, f32[56,512]{1,0:T(8,128)S(1)}, u32[]{:S(2)}, u32[]{:S(2)}) collective-permute-start(f32[56,512]{1,0:T(8,128)S(1)} %get-tuple-element.10), channel_id=1, source_target_pairs={{0,3},{1,2},{2,1},{3,0},{4,7},{5,6},{6,5},{7,4},{8,11},{9,10},{10,... | collective-permute-start | bytes 344072 | tf_op jit(solution)/shard_map/ppermute | solution.py:303
  10.1 0.6 collective-permute-done
  10.7 3.4 %collective-permute-start.1 = (f32[56,512]{1,0:T(8,128)S(1)}, f32[56,512]{1,0:T(8,128)S(1)}, u32[]{:S(2)}, u32[]{:S(2)}) collective-permute-start(f32[56,512]{1,0:T(8,128)S(1)} %add.6.refs_0_), channel_id=1, source_target_pairs={{0,3},{1,2},{2,1},{3,0},{4,7},{5,6},{6,5},{7,4},{8,11},{9,10},{10,... | collective-permute-start | bytes 344072 | tf_op jit(solution)/shard_map/ppermute | solution.py:303
  14.1 0.0 collective-permute-done.2
  14.1 0.1 collective-permute-start.3
  14.2 2.1 %collective-permute-done.1.refs_1_ = f32[56,512]{1,0:T(8,128)S(1)} collective-permute-done((f32[56,512]{1,0:T(8,128)S(1)}, f32[56,512]{1,0:T(8,128)S(1)}, u32[]{:S(2)}, u32[]{:S(2)}) %collective-permute-start.1) | collective-permute-done | bytes 114720 | tf_op jit(solution)/shard_map/ppermute | solution.py:303
  16.3 1.9 %collective-permute-done.3.refs_3_ = f32[56,512]{1,0:T(8,128)S(1)} collective-permute-done((f32[56,512]{1,0:T(8,128)S(1)}, f32[56,512]{1,0:T(8,128)S(1)}, u32[]{:S(2)}, u32[]{:S(2)}) %collective-permute-start.3) | collective-permute-done | bytes 114720 | tf_op jit(solution)/shard_map/ppermute | solution.py:302
  18.1 1.8 %dispatch.1 = (bf16[1024,128]{1,0:T(8,128)(2,1)S(1)}, bf16[128,512]{1,0:T(8,128)(2,1)S(1)}, f32[6,512]{1,0:T(8,128)}) custom-call(f32[56,512]{1,0:T(8,128)S(1)} %add.6.refs_0_, f32[56,512]{1,0:T(8,128)S(1)} %collective-permute-done.1.refs_1_, f32[56,512]{1,0:T(8,128)S(1)} %add.7.refs_2_, f32[56,512]{1,0:T(8,128)S(1)} %collective-permute-done.3.refs_3_, ...), custom_call_target="tpu_custom_call" | custom-call | tf_op jit(solution)/shard_map/dispatch/pallas_call | solution.py:144
  19.9 21.0 %all_to_all.20 = bf16[128,8,128]{2,1,0:T(8,128)(2,1)S(1)} all-to-all(bf16[128,8,128]{2,1,0:T(8,128)(2,1)S(1)} %bitcast.7), channel_id=1, replica_groups=mesh['dp'=32,'tensor'=4] {'dp','tensor'}, dimensions={0} | all-to-all | bytes 524288 | tf_op jit(solution)/shard_map/all_to_all | solution.py:296
  40.9 0.4 merge.1
  41.2 12.7 %all_to_all.21.got_ref = bf16[32,32,128]{2,1,0:T(8,128)(2,1)S(1)} all-to-all(bf16[32,32,128]{2,1,0:T(8,128)(2,1)S(1)} %merge.1), channel_id=1, replica_groups=mesh['dp'=32,'tensor'=4] {'dp'}, dimensions={0} | all-to-all | bytes 524288 | tf_op jit(solution)/shard_map/all_to_all | solution.py:309
  53.9 0.0 copy-done.2
  53.9 0.0 copy-done
  53.9 0.0 copy-done.1
  53.9 2.8 %expert.1 = bf16[1024,128]{1,0:T(8,128)(2,1)S(1)} custom-call(bf16[32,32,128]{2,1,0:T(8,128)(2,1)S(1)} %all_to_all.21.got_ref, bf16[1,448,4096]{2,1,0:T(8,128)(2,1)S(1)} %copy-done, bf16[1,448,4096]{2,1,0:T(8,128)(2,1)S(1)} %copy-done.1, bf16[1,448,4096]{2,1,0:T(8,128)(2,1)S(1)} %copy-done.2), custom_call_target="tpu_custom_call" | custom-call | tf_op jit(solution)/shard_map/expert/pallas_call | solution.py:245
  56.8 14.9 %all_to_all.22 = bf16[128,8,128]{2,1,0:T(8,128)(2,1)S(1)} all-to-all(bf16[128,8,128]{2,1,0:T(8,128)(2,1)S(1)} %bitcast.4), channel_id=1, replica_groups=mesh['dp'=32,'tensor'=4] {'dp','tensor'}, dimensions={0} | all-to-all | bytes 524288 | tf_op jit(solution)/shard_map/all_to_all | solution.py:296
  71.7 0.1 add_up.1
  71.8 12.7 %all_to_all.23.got_ref = bf16[32,32,128]{2,1,0:T(8,128)(2,1)S(1)} all-to-all(bf16[32,32,128]{2,1,0:T(8,128)(2,1)S(1)} %add_up.1), channel_id=1, replica_groups=mesh['dp'=32,'tensor'=4] {'dp'}, dimensions={0} | all-to-all | bytes 524288 | tf_op jit(solution)/shard_map/all_to_all | solution.py:312
  84.4 3.1 %mix.1 = bf16[6,512,1024]{2,1,0:T(8,128)(2,1)} custom-call(bf16[32,32,128]{2,1,0:T(8,128)(2,1)S(1)} %all_to_all.23.got_ref, bf16[128,512]{1,0:T(8,128)(2,1)S(1)} %get-tuple-element.14.combine_ref), custom_call_target="tpu_custom_call" | custom-call | tf_op jit(solution)/shard_map/mix/pallas_call | solution.py:278
  (4 shorter events, 0.0 us)
Async XLA Ops:
  0.6 0.8 copy-start.3
  1.4 52.5 %copy-start.2 = (bf16[1,448,4096]{2,1,0:T(8,128)(2,1)S(1)}, bf16[1,448,4096]{2,1,0:T(8,128)(2,1)}, u32[]{:S(2)}) copy-start(bf16[1,448,4096]{2,1,0:T(8,128)(2,1)} %down_ref.1) | copy-start | bytes 11010052
  5.3 5.4 %collective-permute-start = (f32[56,512]{1,0:T(8,128)S(1)}, f32[56,512]{1,0:T(8,128)S(1)}, u32[]{:S(2)}, u32[]{:S(2)}) collective-permute-start(f32[56,512]{1,0:T(8,128)S(1)} %get-tuple-element.9), channel_id=1, source_target_pairs={{0,1},{1,0},{2,3},{3,2},{4,5},{5,4},{6,7},{7,6},{8,9},{9,8},{10,11... | collective-permute-start | bytes 344072 | tf_op jit(solution)/shard_map/ppermute | solution.py:302
  7.8 6.2 %collective-permute-start.2 = (f32[56,512]{1,0:T(8,128)S(1)}, f32[56,512]{1,0:T(8,128)S(1)}, u32[]{:S(2)}, u32[]{:S(2)}) collective-permute-start(f32[56,512]{1,0:T(8,128)S(1)} %get-tuple-element.10), channel_id=1, source_target_pairs={{0,3},{1,2},{2,1},{3,0},{4,7},{5,6},{6,5},{7,4},{8,11},{9,10},{10,... | collective-permute-start | bytes 344072 | tf_op jit(solution)/shard_map/ppermute | solution.py:303
  10.7 5.5 %collective-permute-start.1 = (f32[56,512]{1,0:T(8,128)S(1)}, f32[56,512]{1,0:T(8,128)S(1)}, u32[]{:S(2)}, u32[]{:S(2)}) collective-permute-start(f32[56,512]{1,0:T(8,128)S(1)} %add.6.refs_0_), channel_id=1, source_target_pairs={{0,3},{1,2},{2,1},{3,0},{4,7},{5,6},{6,5},{7,4},{8,11},{9,10},{10,... | collective-permute-start | bytes 344072 | tf_op jit(solution)/shard_map/ppermute | solution.py:303
  14.1 4.0 %collective-permute-start.3 = (f32[56,512]{1,0:T(8,128)S(1)}, f32[56,512]{1,0:T(8,128)S(1)}, u32[]{:S(2)}, u32[]{:S(2)}) collective-permute-start(f32[56,512]{1,0:T(8,128)S(1)} %add.7.refs_2_), channel_id=1, source_target_pairs={{0,1},{1,0},{2,3},{3,2},{4,5},{5,4},{6,7},{7,6},{8,9},{9,8},{10,11... | collective-permute-start | bytes 344072 | tf_op jit(solution)/shard_map/ppermute | solution.py:302
  18.1 35.8 %copy-start = (bf16[1,448,4096]{2,1,0:T(8,128)(2,1)S(1)}, bf16[1,448,4096]{2,1,0:T(8,128)(2,1)}, u32[]{:S(2)}) copy-start(bf16[1,448,4096]{2,1,0:T(8,128)(2,1)} %gate_ref.1) | copy-start | bytes 11010052
  18.1 35.8 %copy-start.1 = (bf16[1,448,4096]{2,1,0:T(8,128)(2,1)S(1)}, bf16[1,448,4096]{2,1,0:T(8,128)(2,1)}, u32[]{:S(2)}) copy-start(bf16[1,448,4096]{2,1,0:T(8,128)(2,1)} %up_ref.1) | copy-start | bytes 11010052

commit v3 on v2

--- a/solution.py
+++ b/solution.py
@@ -19,7 +19,9 @@
 FULL = 4096
 HID = 448
 HALF = GROUPS // 2
-LROWS = HALF * WS + PAD
+AROWS = HALF * WS + PAD
+BROWS = HALF * WS
+PIECE = 4 * GROUPS
 
 CHUNK = 256
 
@@ -44,11 +46,10 @@
     ]
     for copy in copies:
         copy.start()
+    first_ref[BROWS:, :] = jnp.zeros((PAD, TOK), f32)
     fetch.wait()
     for g in range(GROUPS):
         out_ref, h = (first_ref, second_ref)[g // HALF], g % HALF
-        if h == 0:
-            out_ref[HALF * WS:, :] = jnp.zeros((PAD, TOK), f32)
         copies[g].wait()
         tok = held[g][...]
         out_ref[h * WS:(h + 1) * WS, :] = lax.dot_general(
@@ -58,22 +59,25 @@
         for t in range(TILES):
             part = tok[:, t * LANES:(t + 1) * LANES].astype(f32)
             total += part * part
-        out_ref[HALF * WS + h:HALF * WS + h + 1, :] = jnp.sum(total.T, axis=0, keepdims=True)
+        first_ref[BROWS + g:BROWS + g + 1, :] = jnp.sum(total.T, axis=0, keepdims=True)
 
 
 def partial_logits(tokens, router):
-    logits = jax.ShapeDtypeStruct((LROWS, TOK), f32)
-    held = jax.ShapeDtypeStruct((HALF, TOK, WIDTH), tokens.dtype)
+    first = pltpu.VMEM((AROWS, TOK), f32)
+    second = pltpu.VMEM((BROWS, TOK), f32)
+    held = pltpu.VMEM((HALF, TOK, WIDTH), tokens.dtype)
+    tokens = pltpu.with_memory_space_constraint(tokens, pltpu.HBM)
+    router = pltpu.with_memory_space_constraint(router, pltpu.HBM)
     return pl.pallas_call(
         logits_kernel,
         in_specs=[HBM, HBM],
         out_specs=[VM] * 4,
-        out_shape=[logits, logits, held, held],
+        out_shape=[first, second, held, held],
         scratch_shapes=[
             pltpu.VMEM(router.shape, router.dtype),
             pltpu.SemaphoreType.DMA((GROUPS + 1,)),
         ],
-        compiler_params=params(46),
+        compiler_params=params(54),
         name="partial_logits",
     )(tokens, router)
 
@@ -85,38 +89,31 @@
     return high, mid, rest - mid
 
 
-def spread_rows(ref, rows, value):
-    for n in range(TOK // LANES):
-        ref[n, rows, :] = value[:, n * LANES:(n + 1) * LANES]
+def sum_logits(parts):
+    first = parts[0][...] + parts[1][...]
+    second = parts[2][...] + parts[3][...]
+    scale = lax.rsqrt(first[BROWS:] * (1.0 / FULL) + epsilon)
+    for g in range(GROUPS):
+        half, h = divmod(g, HALF)
+        norm = scale[g:g + 1]
+        yield g, norm, (first, second)[half][h * WS:(h + 1) * WS] * norm
 
 
 def dispatch_kernel(*refs):
-    parts, (held_a, held_b, send_ref, combine_ref, log_ref, wts, cmb, peaks, sums) = refs[:4], refs[4:]
+    parts, (held_a, held_b, send_ref, combine_ref, log_ref, wts, peaks, sums, columns) = refs[:4], refs[4:]
     wts[...] = jnp.zeros_like(wts)
-    cmb[...] = jnp.zeros_like(cmb)
     peaks[...] = jnp.zeros_like(peaks)
     sums[...] = jnp.zeros_like(sums)
-    totals = [parts[0][...] + parts[1][...], parts[2][...] + parts[3][...]]
-    scales = [lax.rsqrt(total[HALF * WS:] * (1.0 / FULL) + epsilon) for total in totals]
-    for g in range(GROUPS):
-        half, h = divmod(g, HALF)
+    columns[...] = jnp.zeros_like(columns)
+    for g, norm, logits in sum_logits(parts):
         rows = pl.ds(g, WS, stride=PAD)
-        norm = scales[half][h:h + 1]
-        logits = totals[half][h * WS:(h + 1) * WS] * norm
         peak = jnp.max(logits, axis=1, keepdims=True)
         powers = jnp.exp(logits - peak)
-        spread_rows(wts, rows, powers * norm)
+        weights = powers * norm
+        for n in range(TOK // LANES):
+            wts[n, rows, :] = weights[:, n * LANES:(n + 1) * LANES]
         peaks[rows, :] = jnp.broadcast_to(peak, (WS, LANES))
         sums[rows, :] = jnp.broadcast_to(jnp.sum(powers, axis=1, keepdims=True), (WS, LANES))
-        row_peak = jnp.max(logits, axis=0, keepdims=True)
-        row_powers = jnp.exp(logits - row_peak)
-        row_sum = jnp.sum(row_powers, axis=0, keepdims=True)
-        spread_rows(cmb, rows, row_powers / row_sum)
-        log_ref[g:g + 1, :] = row_peak + jnp.log(row_sum)
-    combine = jnp.concatenate([cmb[n] for n in range(TOK // LANES)], axis=1)
-    combine_ref[...] = jnp.concatenate(
-        [combine[(4 * k + s) * PAD:(4 * k + s + 1) * PAD] for s in range(SLOTS) for k in range(EXPERTS)]
-    ).astype(bf16)
     weights = jnp.concatenate([wts[n] for n in range(TOK // LANES)], axis=1).astype(bf16)
     group = lax.broadcasted_iota(jnp.int32, (WS * PAD, TOK), 0) % PAD
     acc = jnp.zeros((WS * PAD, WIDTH), f32)
@@ -139,6 +136,21 @@
             )
             send_ref[pl.ds((s * TILES + t) * EXPERTS * PAD, EXPERTS * PAD), :] = block.astype(bf16)
 
+    for g, _, logits in sum_logits(parts):
+        row_peak = jnp.max(logits, axis=0, keepdims=True)
+        row_powers = jnp.exp(logits - row_peak)
+        row_sum = jnp.sum(row_powers, axis=0, keepdims=True)
+        combine = row_powers / row_sum
+        log_ref[g:g + 1, :] = row_peak + jnp.log(row_sum)
+        for n in range(TOK // LANES):
+            for k in range(EXPERTS):
+                rows = pl.ds(k * GROUPS + g, SLOTS, stride=PIECE)
+                columns[g % 2, n, rows, :] = combine[k * SLOTS:(k + 1) * SLOTS, n * LANES:(n + 1) * LANES]
+            combine_ref[g, n * LANES:(n + 1) * LANES, :] = columns[g % 2, n].T.astype(bf16)
+            for k in range(EXPERTS):
+                rows = pl.ds(k * GROUPS + g, SLOTS, stride=PIECE)
+                columns[g % 2, n, rows, :] = jnp.zeros((SLOTS, LANES), f32)
+
 
 def dispatch(parts, held):
     return pl.pallas_call(
@@ -147,14 +159,14 @@
         out_specs=[VM] * 3,
         out_shape=[
             jax.ShapeDtypeStruct((SLOTS * TILES * EXPERTS * PAD, LANES), bf16),
-            jax.ShapeDtypeStruct((WS * PAD, TOK), bf16),
+            jax.ShapeDtypeStruct((GROUPS, TOK, LANES), bf16),
             jax.ShapeDtypeStruct((GROUPS, TOK), f32),
         ],
         scratch_shapes=[
             pltpu.VMEM((TOK // LANES, WS * PAD, LANES), f32),
-            pltpu.VMEM((TOK // LANES, WS * PAD, LANES), f32),
             pltpu.VMEM((WS * PAD, LANES), f32),
             pltpu.VMEM((WS * PAD, LANES), f32),
+            pltpu.VMEM((2, TOK // LANES, LANES, LANES), f32),
         ],
         compiler_params=params(20),
         name="dispatch",
@@ -180,7 +192,7 @@
         for z in range(4):
             row = (i * 4 + z) * PAD
             acc[z] += by * wide[row:row + PAD, :]
-    block = jnp.concatenate(acc).astype(bf16)
+    block = jnp.concatenate([part[:GROUPS] for part in acc]).astype(bf16)
     for i in range(32):
         out_ref[i] = block
 
@@ -190,7 +202,7 @@
     acc = got_ref[0:rows, :].astype(f32)
     for i in range(1, 32):
         acc += got_ref[i * rows:(i + 1) * rows, :].astype(f32)
-    block = acc.astype(bf16)
+    block = jnp.concatenate([acc[k * PAD:k * PAD + GROUPS] for k in range(4)]).astype(bf16)
     for i in range(32):
         out_ref[i] = block
 
@@ -200,7 +212,7 @@
         merge_kernel,
         in_specs=[VM],
         out_specs=VM,
-        out_shape=jax.ShapeDtypeStruct((32, 4 * PAD, LANES), bf16),
+        out_shape=jax.ShapeDtypeStruct((32, PIECE, LANES), bf16),
         scratch_shapes=[pltpu.VMEM((32 * 4 * PAD, LANES), f32)],
         compiler_params=params(8),
         name="merge",
@@ -212,19 +224,20 @@
         add_kernel,
         in_specs=[VM],
         out_specs=VM,
-        out_shape=jax.ShapeDtypeStruct((32, 4 * PAD, LANES), bf16),
+        out_shape=jax.ShapeDtypeStruct((32, PIECE, LANES), bf16),
         compiler_params=params(8),
         name="add_up",
     )(got)
 
 
 def expert_kernel(got_ref, gate_ref, up_ref, down_ref, send_ref, rows):
+    rows[...] = jnp.zeros_like(rows)
     for s in range(SLOTS):
         for t in range(TILES):
             block = got_ref[s * TILES + t].astype(f32)
             for z in range(4):
                 at = (z * TILES + t) * LANES
-                rows[s * PAD:(s + 1) * PAD, at:at + LANES] = block[z * PAD:(z + 1) * PAD]
+                rows[s * PAD:s * PAD + GROUPS, at:at + LANES] = block[z * GROUPS:(z + 1) * GROUPS]
     slot_in = rows[...].astype(bf16)
     gate = lax.dot_general(slot_in, gate_ref[0], NT, preferred_element_type=f32)
     up = lax.dot_general(slot_in, up_ref[0], NT, preferred_element_type=f32)
@@ -253,20 +266,20 @@
     )(got, w_gate, w_up, w_down)
 
 
-def mix_kernel(got_ref, combine_ref, out_ref, slots, turned, block, left):
+def mix_kernel(got_ref, combine_ref, out_ref, rows, slots, block, left):
+    rows[SLOTS * PIECE:, :] = jnp.zeros((LANES - SLOTS * PIECE, WIDTH), f32)
     for s in range(SLOTS):
         for t in range(TILES):
-            slots[s * 32:(s + 1) * 32, t * LANES:(t + 1) * LANES] = got_ref[s * TILES + t]
-    turned[...] = combine_ref[...].astype(f32).T
-    lane = lax.broadcasted_iota(jnp.int32, (CHUNK, WS * PAD), 1) % PAD
+            rows[s * PIECE:(s + 1) * PIECE, t * LANES:(t + 1) * LANES] = got_ref[s * TILES + t].astype(f32)
+    slots[...] = rows[...].astype(bf16)
     copies = []
     for g in range(GROUPS):
         for c in range(TOK // CHUNK):
-            rows = pl.ds(c * CHUNK, CHUNK)
-            mine = jnp.where(lane == g, turned[rows, :], 0.0).astype(bf16)
-            block[g, rows, :] = jnp.dot(mine, slots[...], preferred_element_type=f32).astype(bf16)
+            part = pl.ds(c * CHUNK, CHUNK)
+            mixed = jnp.dot(combine_ref[g, part, :], slots[...], preferred_element_type=f32)
+            block[g, part, :] = mixed.astype(bf16)
             copy = pltpu.make_async_copy(
-                block.at[g, rows], out_ref.at[g, rows], left.at[len(copies)]
+                block.at[g, part], out_ref.at[g, part], left.at[len(copies)]
             )
             copy.start()
             copies.append(copy)
@@ -281,8 +294,8 @@
         out_specs=HBM,
         out_shape=jax.ShapeDtypeStruct((GROUPS, TOK, WIDTH), bf16),
         scratch_shapes=[
-            pltpu.VMEM((WS * PAD, WIDTH), bf16),
-            pltpu.VMEM((TOK, WS * PAD), f32),
+            pltpu.VMEM((LANES, WIDTH), f32),
+            pltpu.VMEM((LANES, WIDTH), bf16),
             pltpu.VMEM((GROUPS, TOK, WIDTH), bf16),
             pltpu.SemaphoreType.DMA((GROUPS * TOK // CHUNK,)),
         ],

time: 87.8 us -> 85.5 us (0.974)
  blocking collectives: 61.3 us -> 59.9 us
    ppermute x2, waiting for transfers between devices: 2.07 us -> 0.01 us  [per_device(): far = lambda x: lax.ppermute(x, 'tensor', [(i, i ^ 3) for i in range(4)])]
    ppermute x2, waiting for transfers between devices: 2.47 us -> 4.36 us  [per_device(): near = lambda x: lax.ppermute(x, 'tensor', [(i, i ^ 1) for i in range(4)])]
  transfers between devices with their start and end apart: 4 -> 4, of which waited for: 3 -> 2; matrix products, arithmetic and copies ran while one was open for 0% -> 0% of each run, Pallas kernels for 0% -> 0%
where the time goes in v3:
time: 85.5 us; the launch traced here: 85.3 us
  blocking collectives  59.9 us (70%)
  Pallas kernels  12.1 us (14%)
  starting transfers between devices  8.24 us (10%)
  waiting for transfers between devices  4.36 us (5%)
    all_to_all x2, blocking collectives, everyone(): x = lax.all_to_all(x, ('dp', 'tensor'), 0, 0, tiled=True)  35.8 us
    all_to_all x1, blocking collectives, per_device(): slot_in = lax.all_to_all(spread, 'dp', 0, 0, tiled=True)  12 us
    all_to_all x1, blocking collectives, per_device(): slot_out = lax.all_to_all(spread, 'dp', 0, 0, tiled=True)  12 us
    ppermute x2, starting transfers between devices, per_device(): far = lambda x: lax.ppermute(x, 'tensor', [(i, i ^ 3) for i in range(4)])  5.61 us
    ppermute x2, waiting for transfers between devices, per_device(): near = lambda x: lax.ppermute(x, 'tensor', [(i, i ^ 1) for i in range(4)])  4.36 us
    pallas_call x1, Pallas kernels, partial_logits(): pl.pallas_call(logits_kernel, in_specs=[HBM, HBM], out_specs=[VM] * 4, ou...  3.89 us
    pallas_call x1, Pallas kernels, mix(): pl.pallas_call(mix_kernel, in_specs=[VM, VM], out_specs=HBM, out_shape=ja...  3.03 us
    pallas_call x1, Pallas kernels, expert(): pl.pallas_call(expert_kernel, in_specs=[VM] * 4, out_specs=VM, out_shape=...  2.85 us
  transfers between devices with their start and end apart: 4, of which 2 were waited for; matrix products, arithmetic and copies ran while one was open for 0% of the time, Pallas kernels for 0%

profile of v3, /device:TPU:1, one launch (start us, length us, event | category | flops | bytes accessed | tf_op | source)
XLA Modules:
  0.0 85.3 jit_solution(12648607308398199537)
XLA Ops:
  0.6 0.0 copy-start.2
  0.6 3.9 %partial_logits.1 = (f32[56,512]{1,0:T(8,128)S(1)}, f32[48,512]{1,0:T(8,128)S(1)}, bf16[3,512,1024]{2,1,0:T(8,128)(2,1)S(1)}, bf16[3,512,1024]{2,1,0:T(8,128)(2,1)S(1)}) custom-call(bf16[6,512,1024]{2,1,0:T(8,128)(2,1)} %tokens_ref.1, bf16[16,1024]{1,0:T(8,128)(2,1)} %router_ref.1), custom_call_target="tpu_custom_call" | custom-call | tf_op jit(solution)/shard_map/partial_logits/pallas_call | solution.py:71
  4.5 2.5 %collective-permute-start = (f32[56,512]{1,0:T(8,128)S(1)}, f32[56,512]{1,0:T(8,128)S(1)}, u32[]{:S(2)}, u32[]{:S(2)}) collective-permute-start(f32[56,512]{1,0:T(8,128)S(1)} %get-tuple-element.9), channel_id=1, source_target_pairs={{0,1},{1,0},{2,3},{3,2},{4,5},{5,4},{6,7},{7,6},{8,9},{9,8},{10,11... | collective-permute-start | bytes 344072 | tf_op jit(solution)/shard_map/ppermute | solution.py:315
  7.1 2.2 %collective-permute-start.2 = (f32[48,512]{1,0:T(8,128)S(1)}, f32[48,512]{1,0:T(8,128)S(1)}, u32[]{:S(2)}, u32[]{:S(2)}) collective-permute-start(f32[48,512]{1,0:T(8,128)S(1)} %get-tuple-element.10), channel_id=1, source_target_pairs={{0,3},{1,2},{2,1},{3,0},{4,7},{5,6},{6,5},{7,4},{8,11},{9,10},{10,... | collective-permute-start | bytes 294920 | tf_op jit(solution)/shard_map/ppermute | solution.py:316
  9.3 0.6 collective-permute-done
  10.0 3.4 %collective-permute-start.1 = (f32[56,512]{1,0:T(8,128)S(1)}, f32[56,512]{1,0:T(8,128)S(1)}, u32[]{:S(2)}, u32[]{:S(2)}) collective-permute-start(f32[56,512]{1,0:T(8,128)S(1)} %add.6.refs_0_), channel_id=1, source_target_pairs={{0,3},{1,2},{2,1},{3,0},{4,7},{5,6},{6,5},{7,4},{8,11},{9,10},{10,... | collective-permute-start | bytes 344072 | tf_op jit(solution)/shard_map/ppermute | solution.py:316
  13.3 0.0 collective-permute-done.2
  13.3 0.1 collective-permute-start.3
  13.4 3.7 %collective-permute-done.3.refs_3_ = f32[48,512]{1,0:T(8,128)S(1)} collective-permute-done((f32[48,512]{1,0:T(8,128)S(1)}, f32[48,512]{1,0:T(8,128)S(1)}, u32[]{:S(2)}, u32[]{:S(2)}) %collective-permute-start.3) | collective-permute-done | bytes 98336 | tf_op jit(solution)/shard_map/ppermute | solution.py:315
  17.2 0.0 collective-permute-done.1.refs_1_
  17.2 0.0 copy-start
  17.2 0.0 copy-start.1
  17.2 1.9 %dispatch.1 = (bf16[1024,128]{1,0:T(8,128)(2,1)S(1)}, bf16[6,512,128]{2,1,0:T(8,128)(2,1)S(1)}, f32[6,512]{1,0:T(8,128)}) custom-call(f32[56,512]{1,0:T(8,128)S(1)} %add.6.refs_0_, f32[56,512]{1,0:T(8,128)S(1)} %collective-permute-done.1.refs_1_, f32[48,512]{1,0:T(8,128)S(1)} %add.7.refs_2_, f32[48,512]{1,0:T(8,128)S(1)} %collective-permute-done.3.refs_3_, ...), custom_call_target="tpu_custom_call" | custom-call | tf_op jit(solution)/shard_map/dispatch/pallas_call | solution.py:156
  19.1 20.8 %all_to_all.20 = bf16[128,8,128]{2,1,0:T(8,128)(2,1)S(1)} all-to-all(bf16[128,8,128]{2,1,0:T(8,128)(2,1)S(1)} %bitcast.7), channel_id=1, replica_groups=mesh['dp'=32,'tensor'=4] {'dp','tensor'}, dimensions={0} | all-to-all | bytes 524288 | tf_op jit(solution)/shard_map/all_to_all | solution.py:309
  39.9 0.4 merge.1
  40.3 12.0 %all_to_all.21.got_ref = bf16[32,24,128]{2,1,0:T(8,128)(2,1)S(1)} all-to-all(bf16[32,24,128]{2,1,0:T(8,128)(2,1)S(1)} %merge.1), channel_id=1, replica_groups=mesh['dp'=32,'tensor'=4] {'dp'}, dimensions={0} | all-to-all | bytes 393216 | tf_op jit(solution)/shard_map/all_to_all | solution.py:322
  52.3 0.0 copy-done.2
  52.3 0.0 copy-done
  52.3 0.0 copy-done.1
  52.3 2.8 %expert.1 = bf16[1024,128]{1,0:T(8,128)(2,1)S(1)} custom-call(bf16[32,24,128]{2,1,0:T(8,128)(2,1)S(1)} %all_to_all.21.got_ref, bf16[1,448,4096]{2,1,0:T(8,128)(2,1)S(1)} %copy-done, bf16[1,448,4096]{2,1,0:T(8,128)(2,1)S(1)} %copy-done.1, bf16[1,448,4096]{2,1,0:T(8,128)(2,1)S(1)} %copy-done.2), custom_call_target="tpu_custom_call" | custom-call | tf_op jit(solution)/shard_map/expert/pallas_call | solution.py:258
  55.2 15.0 %all_to_all.22 = bf16[128,8,128]{2,1,0:T(8,128)(2,1)S(1)} all-to-all(bf16[128,8,128]{2,1,0:T(8,128)(2,1)S(1)} %bitcast.4), channel_id=1, replica_groups=mesh['dp'=32,'tensor'=4] {'dp','tensor'}, dimensions={0} | all-to-all | bytes 524288 | tf_op jit(solution)/shard_map/all_to_all | solution.py:309
  70.2 0.1 add_up.1
  70.2 12.0 %all_to_all.23.got_ref = bf16[32,24,128]{2,1,0:T(8,128)(2,1)S(1)} all-to-all(bf16[32,24,128]{2,1,0:T(8,128)(2,1)S(1)} %add_up.1), channel_id=1, replica_groups=mesh['dp'=32,'tensor'=4] {'dp'}, dimensions={0} | all-to-all | bytes 393216 | tf_op jit(solution)/shard_map/all_to_all | solution.py:325
  82.3 3.0 %mix.1 = bf16[6,512,1024]{2,1,0:T(8,128)(2,1)} custom-call(bf16[32,24,128]{2,1,0:T(8,128)(2,1)S(1)} %all_to_all.23.got_ref, bf16[6,512,128]{2,1,0:T(8,128)(2,1)S(1)} %get-tuple-element.14.combine_ref), custom_call_target="tpu_custom_call" | custom-call | tf_op jit(solution)/shard_map/mix/pallas_call | solution.py:291
  (2 shorter events, 0.0 us)
Async XLA Ops:
  0.6 51.7 %copy-start.2 = (bf16[1,448,4096]{2,1,0:T(8,128)(2,1)S(1)}, bf16[1,448,4096]{2,1,0:T(8,128)(2,1)}, u32[]{:S(2)}) copy-start(bf16[1,448,4096]{2,1,0:T(8,128)(2,1)} %down_ref.1) | copy-start | bytes 11010052
  4.5 5.4 %collective-permute-start = (f32[56,512]{1,0:T(8,128)S(1)}, f32[56,512]{1,0:T(8,128)S(1)}, u32[]{:S(2)}, u32[]{:S(2)}) collective-permute-start(f32[56,512]{1,0:T(8,128)S(1)} %get-tuple-element.9), channel_id=1, source_target_pairs={{0,1},{1,0},{2,3},{3,2},{4,5},{5,4},{6,7},{7,6},{8,9},{9,8},{10,11... | collective-permute-start | bytes 344072 | tf_op jit(solution)/shard_map/ppermute | solution.py:315
  7.1 6.2 %collective-permute-start.2 = (f32[48,512]{1,0:T(8,128)S(1)}, f32[48,512]{1,0:T(8,128)S(1)}, u32[]{:S(2)}, u32[]{:S(2)}) collective-permute-start(f32[48,512]{1,0:T(8,128)S(1)} %get-tuple-element.10), channel_id=1, source_target_pairs={{0,3},{1,2},{2,1},{3,0},{4,7},{5,6},{6,5},{7,4},{8,11},{9,10},{10,... | collective-permute-start | bytes 294920 | tf_op jit(solution)/shard_map/ppermute | solution.py:316
  10.0 7.2 %collective-permute-start.1 = (f32[56,512]{1,0:T(8,128)S(1)}, f32[56,512]{1,0:T(8,128)S(1)}, u32[]{:S(2)}, u32[]{:S(2)}) collective-permute-start(f32[56,512]{1,0:T(8,128)S(1)} %add.6.refs_0_), channel_id=1, source_target_pairs={{0,3},{1,2},{2,1},{3,0},{4,7},{5,6},{6,5},{7,4},{8,11},{9,10},{10,... | collective-permute-start | bytes 344072 | tf_op jit(solution)/shard_map/ppermute | solution.py:316
  13.3 3.8 %collective-permute-start.3 = (f32[48,512]{1,0:T(8,128)S(1)}, f32[48,512]{1,0:T(8,128)S(1)}, u32[]{:S(2)}, u32[]{:S(2)}) collective-permute-start(f32[48,512]{1,0:T(8,128)S(1)} %add.7.refs_2_), channel_id=1, source_target_pairs={{0,1},{1,0},{2,3},{3,2},{4,5},{5,4},{6,7},{7,6},{8,9},{9,8},{10,11... | collective-permute-start | bytes 294920 | tf_op jit(solution)/shard_map/ppermute | solution.py:315
  17.2 35.2 %copy-start = (bf16[1,448,4096]{2,1,0:T(8,128)(2,1)S(1)}, bf16[1,448,4096]{2,1,0:T(8,128)(2,1)}, u32[]{:S(2)}) copy-start(bf16[1,448,4096]{2,1,0:T(8,128)(2,1)} %gate_ref.1) | copy-start | bytes 11010052
  17.2 35.2 %copy-start.1 = (bf16[1,448,4096]{2,1,0:T(8,128)(2,1)S(1)}, bf16[1,448,4096]{2,1,0:T(8,128)(2,1)}, u32[]{:S(2)}) copy-start(bf16[1,448,4096]{2,1,0:T(8,128)(2,1)} %up_ref.1) | copy-start | bytes 11010052

commit v4 on v3

--- a/solution.py
+++ b/solution.py
@@ -24,11 +24,14 @@
 PIECE = 4 * GROUPS
 
 CHUNK = 256
+SPLIT = 1
+SPAN = TOK // SPLIT
 
 epsilon = 1e-05
 bf16 = jnp.bfloat16
 f32 = jnp.float32
 NT = (((1,), (1,)), ((), ()))
+TN = (((0,), (0,)), ((), ()))
 VM = pl.BlockSpec(memory_space=pltpu.VMEM)
 HBM = pl.BlockSpec(memory_space=pltpu.HBM)
 
@@ -39,27 +42,39 @@
 
 def logits_kernel(tokens_ref, router_ref, first_ref, second_ref, held_a, held_b, router, arrived):
     held = [(held_a, held_b)[g // HALF].at[g % HALF] for g in range(GROUPS)]
-    fetch = pltpu.make_async_copy(router_ref, router, arrived.at[GROUPS])
+    fetch = pltpu.make_async_copy(router_ref, router, arrived.at[GROUPS * SPLIT])
     fetch.start()
-    copies = [
-        pltpu.make_async_copy(tokens_ref.at[g], held[g], arrived.at[g]) for g in range(GROUPS)
-    ]
+    copies = []
+    for g in range(GROUPS):
+        for c in range(SPLIT):
+            part = pl.ds(c * SPAN, SPAN)
+            copies.append(
+                pltpu.make_async_copy(
+                    tokens_ref.at[g, part], held[g].at[part], arrived.at[g * SPLIT + c]
+                )
+            )
     for copy in copies:
         copy.start()
     first_ref[BROWS:, :] = jnp.zeros((PAD, TOK), f32)
+    row = lax.broadcasted_iota(jnp.int32, (WS, WS), 0)
+    column = lax.broadcasted_iota(jnp.int32, (WS, WS), 1)
+    swap = (column == (row % EXPERTS) * SLOTS + row // EXPERTS).astype(f32).astype(bf16)
     fetch.wait()
+    slots = jnp.dot(swap, router[...], preferred_element_type=f32).astype(bf16)
     for g in range(GROUPS):
         out_ref, h = (first_ref, second_ref)[g // HALF], g % HALF
-        copies[g].wait()
-        tok = held[g][...]
-        out_ref[h * WS:(h + 1) * WS, :] = lax.dot_general(
-            router[...], tok, NT, preferred_element_type=f32
-        )
-        total = jnp.zeros((TOK, LANES), f32)
-        for t in range(TILES):
-            part = tok[:, t * LANES:(t + 1) * LANES].astype(f32)
-            total += part * part
-        first_ref[BROWS + g:BROWS + g + 1, :] = jnp.sum(total.T, axis=0, keepdims=True)
+        for c in range(SPLIT):
+            copies[g * SPLIT + c].wait()
+            part = slice(c * SPAN, (c + 1) * SPAN)
+            tok = held[g][part, :]
+            out_ref[h * WS:(h + 1) * WS, part] = lax.dot_general(
+                slots, tok, NT, preferred_element_type=f32
+            )
+            total = jnp.zeros((SPAN, LANES), f32)
+            for t in range(TILES):
+                piece = tok[:, t * LANES:(t + 1) * LANES].astype(f32)
+                total += piece * piece
+            first_ref[BROWS + g:BROWS + g + 1, part] = jnp.sum(total.T, axis=0, keepdims=True)
 
 
 def partial_logits(tokens, router):
@@ -75,7 +90,7 @@
         out_shape=[first, second, held, held],
         scratch_shapes=[
             pltpu.VMEM(router.shape, router.dtype),
-            pltpu.SemaphoreType.DMA((GROUPS + 1,)),
+            pltpu.SemaphoreType.DMA((GROUPS * SPLIT + 1,)),
         ],
         compiler_params=params(54),
         name="partial_logits",
@@ -89,31 +104,39 @@
     return high, mid, rest - mid
 
 
-def sum_logits(parts):
+def scaled_logits(parts):
     first = parts[0][...] + parts[1][...]
     second = parts[2][...] + parts[3][...]
     scale = lax.rsqrt(first[BROWS:] * (1.0 / FULL) + epsilon)
-    for g in range(GROUPS):
-        half, h = divmod(g, HALF)
-        norm = scale[g:g + 1]
-        yield g, norm, (first, second)[half][h * WS:(h + 1) * WS] * norm
+    for half, total in enumerate((first, second)):
+        norm = scale[half * HALF:(half + 1) * HALF][:, None, :]
+        yield half, norm, total[:BROWS].reshape(HALF, WS, TOK) * norm
 
 
 def dispatch_kernel(*refs):
-    parts, (held_a, held_b, send_ref, combine_ref, log_ref, wts, peaks, sums, columns) = refs[:4], refs[4:]
+    parts, (held_a, held_b, send_ref, combine_ref, log_ref, wts, peaks, sums) = refs[:4], refs[4:]
     wts[...] = jnp.zeros_like(wts)
     peaks[...] = jnp.zeros_like(peaks)
     sums[...] = jnp.zeros_like(sums)
-    columns[...] = jnp.zeros_like(columns)
-    for g, norm, logits in sum_logits(parts):
-        rows = pl.ds(g, WS, stride=PAD)
-        peak = jnp.max(logits, axis=1, keepdims=True)
+    for half, norm, logits in scaled_logits(parts):
+        peak = jnp.max(logits, axis=2, keepdims=True)
+        row_peak = jnp.max(logits, axis=1, keepdims=True)
         powers = jnp.exp(logits - peak)
+        row_powers = jnp.exp(logits - row_peak)
+        total = jnp.sum(powers, axis=2, keepdims=True)
+        row_sum = jnp.sum(row_powers, axis=1, keepdims=True)
         weights = powers * norm
-        for n in range(TOK // LANES):
-            wts[n, rows, :] = weights[:, n * LANES:(n + 1) * LANES]
-        peaks[rows, :] = jnp.broadcast_to(peak, (WS, LANES))
-        sums[rows, :] = jnp.broadcast_to(jnp.sum(powers, axis=1, keepdims=True), (WS, LANES))
+        combine = (row_powers * (1.0 / row_sum)).astype(bf16)
+        log_total = row_peak + jnp.log(row_sum)
+        for h in range(HALF):
+            g = half * HALF + h
+            rows = pl.ds(g, WS, stride=PAD)
+            for n in range(TOK // LANES):
+                wts[n, rows, :] = weights[h, :, n * LANES:(n + 1) * LANES]
+            peaks[rows, :] = jnp.broadcast_to(peak[h], (WS, LANES))
+            sums[rows, :] = jnp.broadcast_to(total[h], (WS, LANES))
+            combine_ref[g] = combine[h]
+            log_ref[g:g + 1, :] = log_total[h]
     weights = jnp.concatenate([wts[n] for n in range(TOK // LANES)], axis=1).astype(bf16)
     group = lax.broadcasted_iota(jnp.int32, (WS * PAD, TOK), 0) % PAD
     acc = jnp.zeros((WS * PAD, WIDTH), f32)
@@ -131,25 +154,8 @@
     for t in range(TILES):
         tile = jnp.where(member == GROUPS, meta, acc[:, t * LANES:(t + 1) * LANES])
         for s in range(SLOTS):
-            block = jnp.concatenate(
-                [tile[(4 * k + s) * PAD:(4 * k + s + 1) * PAD] for k in range(EXPERTS)]
-            )
+            block = tile[s * EXPERTS * PAD:(s + 1) * EXPERTS * PAD]
             send_ref[pl.ds((s * TILES + t) * EXPERTS * PAD, EXPERTS * PAD), :] = block.astype(bf16)
-
-    for g, _, logits in sum_logits(parts):
-        row_peak = jnp.max(logits, axis=0, keepdims=True)
-        row_powers = jnp.exp(logits - row_peak)
-        row_sum = jnp.sum(row_powers, axis=0, keepdims=True)
-        combine = row_powers / row_sum
-        log_ref[g:g + 1, :] = row_peak + jnp.log(row_sum)
-        for n in range(TOK // LANES):
-            for k in range(EXPERTS):
-                rows = pl.ds(k * GROUPS + g, SLOTS, stride=PIECE)
-                columns[g % 2, n, rows, :] = combine[k * SLOTS:(k + 1) * SLOTS, n * LANES:(n + 1) * LANES]
-            combine_ref[g, n * LANES:(n + 1) * LANES, :] = columns[g % 2, n].T.astype(bf16)
-            for k in range(EXPERTS):
-                rows = pl.ds(k * GROUPS + g, SLOTS, stride=PIECE)
-                columns[g % 2, n, rows, :] = jnp.zeros((SLOTS, LANES), f32)
 
 
 def dispatch(parts, held):
@@ -159,14 +165,13 @@
         out_specs=[VM] * 3,
         out_shape=[
             jax.ShapeDtypeStruct((SLOTS * TILES * EXPERTS * PAD, LANES), bf16),
-            jax.ShapeDtypeStruct((GROUPS, TOK, LANES), bf16),
+            jax.ShapeDtypeStruct((GROUPS, WS, TOK), bf16),
             jax.ShapeDtypeStruct((GROUPS, TOK), f32),
         ],
         scratch_shapes=[
             pltpu.VMEM((TOK // LANES, WS * PAD, LANES), f32),
             pltpu.VMEM((WS * PAD, LANES), f32),
             pltpu.VMEM((WS * PAD, LANES), f32),
-            pltpu.VMEM((2, TOK // LANES, LANES, LANES), f32),
         ],
         compiler_params=params(20),
         name="dispatch",
@@ -197,12 +202,14 @@
         out_ref[i] = block
 
 
-def add_kernel(got_ref, out_ref):
+def add_kernel(got_ref, out_ref, mixed):
     rows = 4 * PAD
     acc = got_ref[0:rows, :].astype(f32)
     for i in range(1, 32):
         acc += got_ref[i * rows:(i + 1) * rows, :].astype(f32)
-    block = jnp.concatenate([acc[k * PAD:k * PAD + GROUPS] for k in range(4)]).astype(bf16)
+    for k in range(EXPERTS):
+        mixed[pl.ds(k, PAD, stride=EXPERTS), :] = acc[k * PAD:(k + 1) * PAD]
+    block = mixed[:PIECE, :].astype(bf16)
     for i in range(32):
         out_ref[i] = block
 
@@ -225,6 +232,7 @@
         in_specs=[VM],
         out_specs=VM,
         out_shape=jax.ShapeDtypeStruct((32, PIECE, LANES), bf16),
+        scratch_shapes=[pltpu.VMEM((EXPERTS * PAD, LANES), f32)],
         compiler_params=params(8),
         name="add_up",
     )(got)
@@ -266,17 +274,23 @@
     )(got, w_gate, w_up, w_down)
 
 
-def mix_kernel(got_ref, combine_ref, out_ref, rows, slots, block, left):
-    rows[SLOTS * PIECE:, :] = jnp.zeros((LANES - SLOTS * PIECE, WIDTH), f32)
+def mix_kernel(got_ref, combine_ref, log_ref, out_ref, log_out, rows, block, left):
+    copies = [pltpu.make_async_copy(log_ref, log_out, left.at[0])]
+    copies[0].start()
     for s in range(SLOTS):
         for t in range(TILES):
-            rows[s * PIECE:(s + 1) * PIECE, t * LANES:(t + 1) * LANES] = got_ref[s * TILES + t].astype(f32)
-    slots[...] = rows[...].astype(bf16)
-    copies = []
+            piece = got_ref[s * TILES + t].astype(f32)
+            for g in range(GROUPS):
+                rows[g, s * EXPERTS:(s + 1) * EXPERTS, t * LANES:(t + 1) * LANES] = piece[
+                    g * EXPERTS:(g + 1) * EXPERTS
+                ]
     for g in range(GROUPS):
+        slots = rows[g].astype(bf16)
         for c in range(TOK // CHUNK):
             part = pl.ds(c * CHUNK, CHUNK)
-            mixed = jnp.dot(combine_ref[g, part, :], slots[...], preferred_element_type=f32)
+            mixed = lax.dot_general(
+                combine_ref[g, :, part], slots, TN, preferred_element_type=f32
+            )
             block[g, part, :] = mixed.astype(bf16)
             copy = pltpu.make_async_copy(
                 block.at[g, part], out_ref.at[g, part], left.at[len(copies)]
@@ -287,21 +301,23 @@
         copy.wait()
 
 
-def mix(got, combine):
+def mix(got, combine, log_total):
     return pl.pallas_call(
         mix_kernel,
-        in_specs=[VM, VM],
-        out_specs=HBM,
-        out_shape=jax.ShapeDtypeStruct((GROUPS, TOK, WIDTH), bf16),
+        in_specs=[VM] * 3,
+        out_specs=[HBM] * 2,
+        out_shape=[
+            jax.ShapeDtypeStruct((GROUPS, TOK, WIDTH), bf16),
+            jax.ShapeDtypeStruct((GROUPS, TOK), f32),
+        ],
         scratch_shapes=[
-            pltpu.VMEM((LANES, WIDTH), f32),
-            pltpu.VMEM((LANES, WIDTH), bf16),
+            pltpu.VMEM((GROUPS, WS, WIDTH), f32),
             pltpu.VMEM((GROUPS, TOK, WIDTH), bf16),
-            pltpu.SemaphoreType.DMA((GROUPS * TOK // CHUNK,)),
+            pltpu.SemaphoreType.DMA((1 + GROUPS * TOK // CHUNK,)),
         ],
         compiler_params=params(24),
         name="mix",
-    )(got, combine)
+    )(got, combine, log_total)
 
 
 def everyone(x):
@@ -323,7 +339,7 @@
     outs = expert(slot_in, w_gate, w_up, w_down)
     spread = add_up(everyone(outs))
     slot_out = lax.all_to_all(spread, "dp", 0, 0, tiled=True)
-    return (mix(slot_out, combine), log_total)
+    return tuple(mix(slot_out, combine, log_total))
 
 
 def solution(mesh):

time: 85.5 us -> 84.9 us (level)
  no operation moved by 1% of the time
where the time goes in v4:
time: 84.9 us; the launch traced here: 84.7 us
  blocking collectives  59.9 us (71%)
  Pallas kernels  11.4 us (13%)
  starting transfers between devices  8.24 us (10%)
  waiting for transfers between devices  4.36 us (5%)
    all_to_all x2, blocking collectives, everyone(): x = lax.all_to_all(x, ('dp', 'tensor'), 0, 0, tiled=True)  35.8 us
    all_to_all x1, blocking collectives, per_device(): slot_out = lax.all_to_all(spread, 'dp', 0, 0, tiled=True)  12 us
    all_to_all x1, blocking collectives, per_device(): slot_in = lax.all_to_all(spread, 'dp', 0, 0, tiled=True)  12 us
    ppermute x2, starting transfers between devices, per_device(): far = lambda x: lax.ppermute(x, 'tensor', [(i, i ^ 3) for i in range(4)])  5.61 us
    ppermute x2, waiting for transfers between devices, per_device(): near = lambda x: lax.ppermute(x, 'tensor', [(i, i ^ 1) for i in range(4)])  4.36 us
    pallas_call x1, Pallas kernels, partial_logits(): pl.pallas_call(logits_kernel, in_specs=[HBM, HBM], out_specs=[VM] * 4, ou...  3.9 us
    pallas_call x1, Pallas kernels, mix(): pl.pallas_call(mix_kernel, in_specs=[VM] * 3, out_specs=[HBM] * 2, out_sh...  3.08 us
    pallas_call x1, Pallas kernels, expert(): pl.pallas_call(expert_kernel, in_specs=[VM] * 4, out_specs=VM, out_shape=...  2.84 us
  transfers between devices with their start and end apart: 4, of which 2 were waited for; matrix products, arithmetic and copies ran while one was open for 0% of the time, Pallas kernels for 0%

profile of v4, /device:TPU:1, one launch (start us, length us, event | category | flops | bytes accessed | tf_op | source)
XLA Modules:
  0.0 84.7 jit_solution(11239130454177493024)
XLA Ops:
  0.6 0.0 copy-start.2
  0.6 3.9 %partial_logits.1 = (f32[56,512]{1,0:T(8,128)S(1)}, f32[48,512]{1,0:T(8,128)S(1)}, bf16[3,512,1024]{2,1,0:T(8,128)(2,1)S(1)}, bf16[3,512,1024]{2,1,0:T(8,128)(2,1)S(1)}) custom-call(bf16[6,512,1024]{2,1,0:T(8,128)(2,1)} %tokens_ref.1, bf16[16,1024]{1,0:T(8,128)(2,1)} %router_ref.1), custom_call_target="tpu_custom_call" | custom-call | tf_op jit(solution)/shard_map/partial_logits/pallas_call | solution.py:86
  4.6 2.5 %collective-permute-start = (f32[56,512]{1,0:T(8,128)S(1)}, f32[56,512]{1,0:T(8,128)S(1)}, u32[]{:S(2)}, u32[]{:S(2)}) collective-permute-start(f32[56,512]{1,0:T(8,128)S(1)} %get-tuple-element.9), channel_id=1, source_target_pairs={{0,1},{1,0},{2,3},{3,2},{4,5},{5,4},{6,7},{7,6},{8,9},{9,8},{10,11... | collective-permute-start | bytes 344072 | tf_op jit(solution)/shard_map/ppermute | solution.py:331
  7.1 2.2 %collective-permute-start.2 = (f32[48,512]{1,0:T(8,128)S(1)}, f32[48,512]{1,0:T(8,128)S(1)}, u32[]{:S(2)}, u32[]{:S(2)}) collective-permute-start(f32[48,512]{1,0:T(8,128)S(1)} %get-tuple-element.10), channel_id=1, source_target_pairs={{0,3},{1,2},{2,1},{3,0},{4,7},{5,6},{6,5},{7,4},{8,11},{9,10},{10,... | collective-permute-start | bytes 294920 | tf_op jit(solution)/shard_map/ppermute | solution.py:332
  9.3 0.6 collective-permute-done
  10.0 3.4 %collective-permute-start.1 = (f32[56,512]{1,0:T(8,128)S(1)}, f32[56,512]{1,0:T(8,128)S(1)}, u32[]{:S(2)}, u32[]{:S(2)}) collective-permute-start(f32[56,512]{1,0:T(8,128)S(1)} %add.6.refs_0_), channel_id=1, source_target_pairs={{0,3},{1,2},{2,1},{3,0},{4,7},{5,6},{6,5},{7,4},{8,11},{9,10},{10,... | collective-permute-start | bytes 344072 | tf_op jit(solution)/shard_map/ppermute | solution.py:332
  13.3 0.0 collective-permute-done.2
  13.4 0.1 collective-permute-start.3
  13.4 3.7 %collective-permute-done.3.refs_3_ = f32[48,512]{1,0:T(8,128)S(1)} collective-permute-done((f32[48,512]{1,0:T(8,128)S(1)}, f32[48,512]{1,0:T(8,128)S(1)}, u32[]{:S(2)}, u32[]{:S(2)}) %collective-permute-start.3) | collective-permute-done | bytes 98336 | tf_op jit(solution)/shard_map/ppermute | solution.py:331
  17.2 0.0 collective-permute-done.1.refs_1_
  17.2 0.0 copy-start
  17.2 0.0 copy-start.1
  17.2 1.2 %dispatch.1 = (bf16[1024,128]{1,0:T(8,128)(2,1)S(1)}, bf16[6,16,512]{2,1,0:T(8,128)(2,1)S(1)}, f32[6,512]{1,0:T(8,128)S(1)}) custom-call(f32[56,512]{1,0:T(8,128)S(1)} %add.6.refs_0_, f32[56,512]{1,0:T(8,128)S(1)} %collective-permute-done.1.refs_1_, f32[48,512]{1,0:T(8,128)S(1)} %add.7.refs_2_, f32[48,512]{1,0:T(8,128)S(1)} %collective-permute-done.3.refs_3_, ...), custom_call_target="tpu_custom_call" | custom-call | tf_op jit(solution)/shard_map/dispatch/pallas_call | solution.py:162
  18.4 20.8 %all_to_all.20 = bf16[128,8,128]{2,1,0:T(8,128)(2,1)S(1)} all-to-all(bf16[128,8,128]{2,1,0:T(8,128)(2,1)S(1)} %bitcast.7), channel_id=1, replica_groups=mesh['dp'=32,'tensor'=4] {'dp','tensor'}, dimensions={0} | all-to-all | bytes 524288 | tf_op jit(solution)/shard_map/all_to_all | solution.py:325
  39.2 0.4 merge.1
  39.6 12.0 %all_to_all.21.got_ref = bf16[32,24,128]{2,1,0:T(8,128)(2,1)S(1)} all-to-all(bf16[32,24,128]{2,1,0:T(8,128)(2,1)S(1)} %merge.1), channel_id=1, replica_groups=mesh['dp'=32,'tensor'=4] {'dp'}, dimensions={0} | all-to-all | bytes 393216 | tf_op jit(solution)/shard_map/all_to_all | solution.py:338
  51.7 0.0 copy-done.2
  51.7 0.0 copy-done
  51.7 0.0 copy-done.1
  51.7 2.8 %expert.1 = bf16[1024,128]{1,0:T(8,128)(2,1)S(1)} custom-call(bf16[32,24,128]{2,1,0:T(8,128)(2,1)S(1)} %all_to_all.21.got_ref, bf16[1,448,4096]{2,1,0:T(8,128)(2,1)S(1)} %copy-done, bf16[1,448,4096]{2,1,0:T(8,128)(2,1)S(1)} %copy-done.1, bf16[1,448,4096]{2,1,0:T(8,128)(2,1)S(1)} %copy-done.2), custom_call_target="tpu_custom_call" | custom-call | tf_op jit(solution)/shard_map/expert/pallas_call | solution.py:266
  54.5 15.0 %all_to_all.22 = bf16[128,8,128]{2,1,0:T(8,128)(2,1)S(1)} all-to-all(bf16[128,8,128]{2,1,0:T(8,128)(2,1)S(1)} %bitcast.4), channel_id=1, replica_groups=mesh['dp'=32,'tensor'=4] {'dp','tensor'}, dimensions={0} | all-to-all | bytes 524288 | tf_op jit(solution)/shard_map/all_to_all | solution.py:325
  69.5 0.1 add_up.1
  69.5 12.0 %all_to_all.23.got_ref = bf16[32,24,128]{2,1,0:T(8,128)(2,1)S(1)} all-to-all(bf16[32,24,128]{2,1,0:T(8,128)(2,1)S(1)} %add_up.1), channel_id=1, replica_groups=mesh['dp'=32,'tensor'=4] {'dp'}, dimensions={0} | all-to-all | bytes 393216 | tf_op jit(solution)/shard_map/all_to_all | solution.py:341
  81.6 3.1 %mix.1 = (bf16[6,512,1024]{2,1,0:T(8,128)(2,1)}, f32[6,512]{1,0:T(8,128)}) custom-call(bf16[32,24,128]{2,1,0:T(8,128)(2,1)S(1)} %all_to_all.23.got_ref, bf16[6,16,512]{2,1,0:T(8,128)(2,1)S(1)} %get-tuple-element.14.combine_ref, f32[6,512]{1,0:T(8,128)S(1)} %get-tuple-element.15.log_ref), custom_call_target="tpu_custom_call" | custom-call | tf_op jit(solution)/shard_map/mix/pallas_call | solution.py:305
  (2 shorter events, 0.0 us)
Async XLA Ops:
  0.6 51.0 %copy-start.2 = (bf16[1,448,4096]{2,1,0:T(8,128)(2,1)S(1)}, bf16[1,448,4096]{2,1,0:T(8,128)(2,1)}, u32[]{:S(2)}) copy-start(bf16[1,448,4096]{2,1,0:T(8,128)(2,1)} %down_ref.1) | copy-start | bytes 11010052
  4.6 5.4 %collective-permute-start = (f32[56,512]{1,0:T(8,128)S(1)}, f32[56,512]{1,0:T(8,128)S(1)}, u32[]{:S(2)}, u32[]{:S(2)}) collective-permute-start(f32[56,512]{1,0:T(8,128)S(1)} %get-tuple-element.9), channel_id=1, source_target_pairs={{0,1},{1,0},{2,3},{3,2},{4,5},{5,4},{6,7},{7,6},{8,9},{9,8},{10,11... | collective-permute-start | bytes 344072 | tf_op jit(solution)/shard_map/ppermute | solution.py:331
  7.1 6.2 %collective-permute-start.2 = (f32[48,512]{1,0:T(8,128)S(1)}, f32[48,512]{1,0:T(8,128)S(1)}, u32[]{:S(2)}, u32[]{:S(2)}) collective-permute-start(f32[48,512]{1,0:T(8,128)S(1)} %get-tuple-element.10), channel_id=1, source_target_pairs={{0,3},{1,2},{2,1},{3,0},{4,7},{5,6},{6,5},{7,4},{8,11},{9,10},{10,... | collective-permute-start | bytes 294920 | tf_op jit(solution)/shard_map/ppermute | solution.py:332
  10.0 7.2 %collective-permute-start.1 = (f32[56,512]{1,0:T(8,128)S(1)}, f32[56,512]{1,0:T(8,128)S(1)}, u32[]{:S(2)}, u32[]{:S(2)}) collective-permute-start(f32[56,512]{1,0:T(8,128)S(1)} %add.6.refs_0_), channel_id=1, source_target_pairs={{0,3},{1,2},{2,1},{3,0},{4,7},{5,6},{6,5},{7,4},{8,11},{9,10},{10,... | collective-permute-start | bytes 344072 | tf_op jit(solution)/shard_map/ppermute | solution.py:332
  13.4 3.8 %collective-permute-start.3 = (f32[48,512]{1,0:T(8,128)S(1)}, f32[48,512]{1,0:T(8,128)S(1)}, u32[]{:S(2)}, u32[]{:S(2)}) collective-permute-start(f32[48,512]{1,0:T(8,128)S(1)} %add.7.refs_2_), channel_id=1, source_target_pairs={{0,1},{1,0},{2,3},{3,2},{4,5},{5,4},{6,7},{7,6},{8,9},{9,8},{10,11... | collective-permute-start | bytes 294920 | tf_op jit(solution)/shard_map/ppermute | solution.py:331
  17.2 34.5 %copy-start = (bf16[1,448,4096]{2,1,0:T(8,128)(2,1)S(1)}, bf16[1,448,4096]{2,1,0:T(8,128)(2,1)}, u32[]{:S(2)}) copy-start(bf16[1,448,4096]{2,1,0:T(8,128)(2,1)} %gate_ref.1) | copy-start | bytes 11010052
  17.2 34.5 %copy-start.1 = (bf16[1,448,4096]{2,1,0:T(8,128)(2,1)S(1)}, bf16[1,448,4096]{2,1,0:T(8,128)(2,1)}, u32[]{:S(2)}) copy-start(bf16[1,448,4096]{2,1,0:T(8,128)(2,1)} %up_ref.1) | copy-start | bytes 11010052
